TPU v7x, 256 devices: a whole 4x4x8 slice. The times are simulated.
256 devices in a mesh: dp: 8 (over y, x_lo), ctx: 8 (over z), head: 4 (over x_hi, core).
Axes of the slice: x: 4 (x_hi: 2, x_lo: 2; x = x_hi * 2 + x_lo), y: 4, z: 8, core: 2. Of those that a mesh axis runs over, the one named last changes fastest.
Arguments:
- queries: bfloat16 [24576, 5120], P(('dp', 'ctx'), 'head'), parts along dimension 0, may hold values from -160 to 160
- keys: bfloat16 [24576, 1024], P(('dp', 'ctx'), 'head'), parts along dimension 0, may hold values from -8 to 8
- values: bfloat16 [24576, 1024], P(('dp', 'ctx'), 'head'), parts along dimension 0, may hold values from -6 to 6
- block_order: int32 [192], P('dp'), parts along dimension 0, may hold values from 0 to 23, as said below
- resp_lengths: int32 [128], P('dp'), parts along dimension 0, may hold values from 1 to 576, 2304 in all
Outputs:
- attended: bfloat16 [192, 128, 5120], P(('dp', 'ctx'), 'head'), parts along dimension 0
- logsumexp: float32 [40, 24576], P('head', ('dp', 'ctx')), parts along dimension 1
There are 8 independent parts, one for each index of `dp`. A program takes and returns all parts, laid end to end along the dimension named above; each array names one. Nothing has to cross between parts.
Inputs may be any that keep to these rules, and one draw needn't show every extreme that they name: block_order is a permutation of the 24 sequence blocks; sequence blocks o * 3 to (o + 1) * 3 - 1 belong to index o of ctx, and the 3 blocks stored on one index of ctx belong to 3 different indices of ctx. `resp_lengths`: the prompt fills the first 768 positions and the 16 responses follow in order, their lengths summing to 2304.
All inputs are finite; a program needn't handle non-finite values.
Results may differ from a plain program's by a relative error of at most 0.012.
Values may be sent and summed in bfloat16 or wider, within the bound.
A program may use at most 64 MiB of HBM per device.

v0:
```python
import math

import jax
import jax.numpy as jnp
from jax import lax
from jax.sharding import PartitionSpec as P

HEAD_FEATURES = 128
MASK_BLOCK_SIZE = 128


def sequence_layout(block_order, resp_lengths):
    within = jnp.arange(MASK_BLOCK_SIZE, dtype=jnp.int32)
    position = (block_order[:, None] * MASK_BLOCK_SIZE + within[None, :]).reshape(-1)
    packed_row_total = position.shape[0]
    prompt = packed_row_total - jnp.sum(resp_lengths)
    resp_ends = prompt + jnp.cumsum(resp_lengths)
    later_ends = jnp.sum((position[:, None] >= resp_ends[None, :]).astype(jnp.int32), axis=1)
    segment = jnp.where(position >= prompt, 1 + later_ends, 0)
    return (position, segment)


def local(queries, keys, values, block_order, resp_lengths):
    local_rows = queries.shape[0]
    heads_q = queries.shape[1] // HEAD_FEATURES
    heads_kv = keys.shape[1] // HEAD_FEATURES
    group_size = heads_q // heads_kv
    score_scale = 1.0 / math.sqrt(HEAD_FEATURES)
    position, segment = sequence_layout(block_order, resp_lengths)
    cycle_index = lax.axis_index("ctx")
    row_start = cycle_index * local_rows
    query_pos = lax.dynamic_slice_in_dim(position, row_start, local_rows)
    query_seg = lax.dynamic_slice_in_dim(segment, row_start, local_rows)
    query_head_tensor = queries.reshape(local_rows, heads_kv, group_size, HEAD_FEATURES)

    def attend_block(carried, key_rows, value_rows, key_start):
        run_max, run_sum, run_acc = carried
        key_count = key_rows.shape[0]
        key_head_tensor = key_rows.reshape(key_count, heads_kv, HEAD_FEATURES)
        value_head_tensor = value_rows.reshape(key_count, heads_kv, HEAD_FEATURES)
        score = (
            jnp.einsum(
                "tkgd,ukd->kgtu",
                query_head_tensor,
                key_head_tensor,
                preferred_element_type=jnp.float32,
            )
            * score_scale
        )
        key_pos = lax.dynamic_slice_in_dim(position, key_start, key_count)
        key_seg = lax.dynamic_slice_in_dim(segment, key_start, key_count)
        allowed = (key_pos[None, :] <= query_pos[:, None]) & (
            (key_seg[None, :] == 0) | (key_seg[None, :] == query_seg[:, None])
        )
        masked = jnp.where(allowed, score, -1e30)
        new_max = jnp.maximum(run_max, jnp.max(masked, axis=-1))
        weights = jnp.where(allowed, jnp.exp(masked - new_max[..., None]), 0.0)
        factor = jnp.exp(run_max - new_max)
        run_sum = run_sum * factor + jnp.sum(weights, axis=-1)
        update = jnp.einsum(
            "kgtu,ukd->kgtd",
            weights.astype(jnp.bfloat16),
            value_head_tensor,
            preferred_element_type=jnp.float32,
        )
        run_acc = run_acc * factor[..., None] + update
        return (new_max, run_sum, run_acc)

    start_max = jnp.full((heads_kv, group_size, local_rows), -1e30, jnp.float32)
    start_sum = jnp.zeros((heads_kv, group_size, local_rows), jnp.float32)
    start_acc = jnp.zeros((heads_kv, group_size, local_rows, HEAD_FEATURES), jnp.float32)
    key_rows = lax.all_gather(keys, "ctx", axis=0, tiled=True)
    value_rows = lax.all_gather(values, "ctx", axis=0, tiled=True)
    key_count = key_rows.shape[0]
    step_count = key_count // local_rows

    def scan_step(state, stacked):
        key_part, value_part, offset = stacked
        return (attend_block(state, key_part, value_part, offset * local_rows), None)

    stacked = (
        key_rows.reshape(step_count, local_rows, key_rows.shape[1]),
        value_rows.reshape(step_count, local_rows, value_rows.shape[1]),
        jnp.arange(step_count, dtype=jnp.int32),
    )
    finished, unused = lax.scan(scan_step, (start_max, start_sum, start_acc), stacked)
    run_max, run_sum, run_acc = finished
    logsumexp = (run_max + jnp.log(run_sum)).reshape(heads_q, local_rows)
    context = (
        (run_acc / run_sum[..., None])
        .transpose(2, 0, 1, 3)
        .reshape(local_rows, heads_q * HEAD_FEATURES)
        .astype(jnp.bfloat16)
    )
    blocks_here = local_rows // MASK_BLOCK_SIZE
    own_blocks = context.reshape(blocks_here, MASK_BLOCK_SIZE, heads_q * HEAD_FEATURES)
    cycle_size = lax.axis_size("ctx")
    slot_count = (blocks_here + cycle_size - 1) // cycle_size
    total_blocks = block_order.shape[0]
    stored_ids = jnp.arange(total_blocks, dtype=jnp.int32)
    stored_dev = stored_ids // blocks_here
    owner_dev = block_order // blocks_here
    earlier = stored_ids[:, None] > stored_ids[None, :]
    same_owner = (
        (stored_dev[:, None] == stored_dev[None, :])
        & (owner_dev[:, None] == owner_dev[None, :])
        & earlier
    )
    slot_rank = jnp.sum(same_owner.astype(jnp.int32), axis=1)
    local_ids = cycle_index * blocks_here + jnp.arange(blocks_here, dtype=jnp.int32)
    dest_slot = jnp.take(owner_dev, local_ids) * slot_count + jnp.take(slot_rank, local_ids)
    inverse = jnp.zeros((total_blocks,), jnp.int32).at[block_order].set(stored_ids)
    wanted = jnp.take(inverse, local_ids)
    source_slot = wanted // blocks_here * slot_count + jnp.take(slot_rank, wanted)
    outgoing = (
        jnp.zeros((cycle_size * slot_count, MASK_BLOCK_SIZE, heads_q * HEAD_FEATURES), jnp.bfloat16)
        .at[dest_slot]
        .set(own_blocks)
    )
    arrived = lax.all_to_all(
        lax.all_to_all(outgoing, "ctx", split_axis=0, concat_axis=0, tiled=True),
        "head",
        split_axis=1,
        concat_axis=2,
        tiled=True,
    )
    attended = jnp.take(arrived, source_slot, axis=0)
    return (attended, logsumexp)


def solution(mesh):
    in_specs = (
        P(("dp", "ctx"), "head"),
        P(("dp", "ctx"), "head"),
        P(("dp", "ctx"), "head"),
        P("dp"),
        P("dp"),
    )
    out_specs = (P(("dp", "ctx"), "head", None), P("head", ("dp", "ctx")))
    return jax.shard_map(local, mesh=mesh, in_specs=in_specs, out_specs=out_specs, check_vma=False)
```

profile of v0, /device:TPU:1, one launch (start us, length us, event | category | flops | bytes accessed | tf_op | source)
XLA Modules:
  0.0 362.7 jit_solution(10956518351272887398)
XLA Ops:
  8.7 1.3 reduce_sum.37
  12.6 1.6 copy.44
  16.4 33.4 %all-gather.3.cloned.1.call-done = bf16[3072,256]{1,0:T(8,128)(2,1)} async-done(((bf16[384,256]{1,0:T(8,128)(2,1)}), bf16[3072,256]{1,0:T(8,128)(2,1)}) %all-gather.3.cloned.1.call-update) | async-done | bytes 1572880 | tf_op jit(solution)/shard_map/all_gather | solution.py:72
  49.8 40.4 %all-gather.5.cloned.1.call-done = bf16[3072,256]{1,0:T(8,128)(2,1)} async-done(((bf16[384,256]{1,0:T(8,128)(2,1)}), bf16[3072,256]{1,0:T(8,128)(2,1)}) %all-gather.5.cloned.1.call-update) | async-done | bytes 1572880 | tf_op jit(solution)/shard_map/all_gather | solution.py:73
  90.2 140.9 %while.15 = (s32[]{:T(128)}, f32[2,5,384]{2,1,0:T(8,128)S(1)}, f32[2,5,384]{2,1,0:T(8,128)S(1)}, f32[2,5,384,128]{3,2,1,0:T(8,128)}, s32[8]{0:T(128)S(1)}, /*ind...) while((s32[]{:T(128)}, f32[2,5,384]{2,1,0:T(8,128)S(1)}, ...), condition=%wide.region_8.10_spmd.clone, body=%wide.region_5.9_spmd.clone.sunk | while | flops 776227968 | bytes 25424872 | solution.py:86
  91.8 1.1 constant_dynamic-slice_fusion.3
  93.0 3.7 %fusion.33 = (f32[2,5,384]{2,1,0:T(8,128)S(1)}, f32[2,384,384,5]{2,1,3,0:T(8,128)}) fusion(pred[384,384]{0,1:T(8,128)(4,1)S(1)} %or_and_fusion.2, bf16[384,2,128,1]{0,2,3,1:T(8,128)(2,1)S(1)} %bitcast.58, bf16[384,2,5,128]{3,0,2,1:T(8,128)(2,1)S(1)} %get-tuple-element.326), kind=kOutput, calls=%fused_computation.9.clone.1 | convolution fusion | flops 381907200 | bytes 7240704 | tf_op jit(solution)/shard_map/while/body/eval_jaxpr/tkgd,ukd->kgtu/dot_general | solution.py:42
  96.8 4.1 %fusion.34 = f32[2,5,384]{2,1,0:T(8,128)S(1)} fusion(f32[2,384,384,5]{2,1,3,0:T(8,128)} %get-tuple-element.280, f32[2,5,384]{2,1,0:T(8,128)S(1)} %select_maximum_fusion.2, pred[384,384]{0,1:T(8,128)(4,1)S(1)} %or_and_fusion.2), kind=kLoop, calls=%fused_computation.11.clone.1 | loop fusion | flops 7368960 | bytes 6076416 | tf_op jit(solution)/shard_map/while/body/eval_jaxpr/reduce_sum | solution.py:59
  101.1 6.2 %fusion.36 = f32[2,5,384,128]{3,2,1,0:T(8,128)} fusion(f32[2,5,384,128]{3,2,1,0:T(8,128)} %get-tuple-element.303, bf16[384,2,128,1]{0,2,3,1:T(8,128)(2,1)S(1)} %bitcast.60, f32[2,384,384,5]{2,1,3,0:T(8,128)} %get-tuple-element.280, f32[2,5,384]{2,1,0:T(8,128)S(1)} %select_maximum_fusion.2, pred[384,384]{0,1:T(8,128)(4,1)S(1)} %or_and_fusion.2, ...), kind=kOutput, calls=%fused_computation.15.clone.1 | convolution fusion | flops 386334720 | bytes 10205185 | tf_op jit(solution)/shard_map/while/body/eval_jaxpr/kgtu,ukd->kgtd/dot_general | solution.py:60
  108.9 1.1 constant_dynamic-slice_fusion.3
  110.1 3.7 %fusion.33 = (f32[2,5,384]{2,1,0:T(8,128)S(1)}, f32[2,384,384,5]{2,1,3,0:T(8,128)}) fusion(pred[384,384]{0,1:T(8,128)(4,1)S(1)} %or_and_fusion.2, bf16[384,2,128,1]{0,2,3,1:T(8,128)(2,1)S(1)} %bitcast.58, bf16[384,2,5,128]{3,0,2,1:T(8,128)(2,1)S(1)} %get-tuple-element.326), kind=kOutput, calls=%fused_computation.9.clone.1 | convolution fusion | flops 381907200 | bytes 7240704 | tf_op jit(solution)/shard_map/while/body/eval_jaxpr/tkgd,ukd->kgtu/dot_general | solution.py:42
  113.9 4.1 %fusion.34 = f32[2,5,384]{2,1,0:T(8,128)S(1)} fusion(f32[2,384,384,5]{2,1,3,0:T(8,128)} %get-tuple-element.280, f32[2,5,384]{2,1,0:T(8,128)S(1)} %select_maximum_fusion.2, pred[384,384]{0,1:T(8,128)(4,1)S(1)} %or_and_fusion.2), kind=kLoop, calls=%fused_computation.11.clone.1 | loop fusion | flops 7368960 | bytes 6076416 | tf_op jit(solution)/shard_map/while/body/eval_jaxpr/reduce_sum | solution.py:59
  118.2 6.8 %fusion.36 = f32[2,5,384,128]{3,2,1,0:T(8,128)} fusion(f32[2,5,384,128]{3,2,1,0:T(8,128)} %get-tuple-element.303, bf16[384,2,128,1]{0,2,3,1:T(8,128)(2,1)S(1)} %bitcast.60, f32[2,384,384,5]{2,1,3,0:T(8,128)} %get-tuple-element.280, f32[2,5,384]{2,1,0:T(8,128)S(1)} %select_maximum_fusion.2, pred[384,384]{0,1:T(8,128)(4,1)S(1)} %or_and_fusion.2, ...), kind=kOutput, calls=%fused_computation.15.clone.1 | convolution fusion | flops 386334720 | bytes 10205185 | tf_op jit(solution)/shard_map/while/body/eval_jaxpr/kgtu,ukd->kgtd/dot_general | solution.py:60
  126.6 1.1 constant_dynamic-slice_fusion.3
  127.8 3.7 %fusion.33 = (f32[2,5,384]{2,1,0:T(8,128)S(1)}, f32[2,384,384,5]{2,1,3,0:T(8,128)}) fusion(pred[384,384]{0,1:T(8,128)(4,1)S(1)} %or_and_fusion.2, bf16[384,2,128,1]{0,2,3,1:T(8,128)(2,1)S(1)} %bitcast.58, bf16[384,2,5,128]{3,0,2,1:T(8,128)(2,1)S(1)} %get-tuple-element.326), kind=kOutput, calls=%fused_computation.9.clone.1 | convolution fusion | flops 381907200 | bytes 7240704 | tf_op jit(solution)/shard_map/while/body/eval_jaxpr/tkgd,ukd->kgtu/dot_general | solution.py:42
  131.6 4.1 %fusion.34 = f32[2,5,384]{2,1,0:T(8,128)S(1)} fusion(f32[2,384,384,5]{2,1,3,0:T(8,128)} %get-tuple-element.280, f32[2,5,384]{2,1,0:T(8,128)S(1)} %select_maximum_fusion.2, pred[384,384]{0,1:T(8,128)(4,1)S(1)} %or_and_fusion.2), kind=kLoop, calls=%fused_computation.11.clone.1 | loop fusion | flops 7368960 | bytes 6076416 | tf_op jit(solution)/shard_map/while/body/eval_jaxpr/reduce_sum | solution.py:59
  135.9 6.8 %fusion.36 = f32[2,5,384,128]{3,2,1,0:T(8,128)} fusion(f32[2,5,384,128]{3,2,1,0:T(8,128)} %get-tuple-element.303, bf16[384,2,128,1]{0,2,3,1:T(8,128)(2,1)S(1)} %bitcast.60, f32[2,384,384,5]{2,1,3,0:T(8,128)} %get-tuple-element.280, f32[2,5,384]{2,1,0:T(8,128)S(1)} %select_maximum_fusion.2, pred[384,384]{0,1:T(8,128)(4,1)S(1)} %or_and_fusion.2, ...), kind=kOutput, calls=%fused_computation.15.clone.1 | convolution fusion | flops 386334720 | bytes 10205185 | tf_op jit(solution)/shard_map/while/body/eval_jaxpr/kgtu,ukd->kgtd/dot_general | solution.py:60
  144.3 1.1 constant_dynamic-slice_fusion.3
  145.5 3.7 %fusion.33 = (f32[2,5,384]{2,1,0:T(8,128)S(1)}, f32[2,384,384,5]{2,1,3,0:T(8,128)}) fusion(pred[384,384]{0,1:T(8,128)(4,1)S(1)} %or_and_fusion.2, bf16[384,2,128,1]{0,2,3,1:T(8,128)(2,1)S(1)} %bitcast.58, bf16[384,2,5,128]{3,0,2,1:T(8,128)(2,1)S(1)} %get-tuple-element.326), kind=kOutput, calls=%fused_computation.9.clone.1 | convolution fusion | flops 381907200 | bytes 7240704 | tf_op jit(solution)/shard_map/while/body/eval_jaxpr/tkgd,ukd->kgtu/dot_general | solution.py:42
  149.2 4.1 %fusion.34 = f32[2,5,384]{2,1,0:T(8,128)S(1)} fusion(f32[2,384,384,5]{2,1,3,0:T(8,128)} %get-tuple-element.280, f32[2,5,384]{2,1,0:T(8,128)S(1)} %select_maximum_fusion.2, pred[384,384]{0,1:T(8,128)(4,1)S(1)} %or_and_fusion.2), kind=kLoop, calls=%fused_computation.11.clone.1 | loop fusion | flops 7368960 | bytes 6076416 | tf_op jit(solution)/shard_map/while/body/eval_jaxpr/reduce_sum | solution.py:59
  153.5 6.8 %fusion.36 = f32[2,5,384,128]{3,2,1,0:T(8,128)} fusion(f32[2,5,384,128]{3,2,1,0:T(8,128)} %get-tuple-element.303, bf16[384,2,128,1]{0,2,3,1:T(8,128)(2,1)S(1)} %bitcast.60, f32[2,384,384,5]{2,1,3,0:T(8,128)} %get-tuple-element.280, f32[2,5,384]{2,1,0:T(8,128)S(1)} %select_maximum_fusion.2, pred[384,384]{0,1:T(8,128)(4,1)S(1)} %or_and_fusion.2, ...), kind=kOutput, calls=%fused_computation.15.clone.1 | convolution fusion | flops 386334720 | bytes 10205185 | tf_op jit(solution)/shard_map/while/body/eval_jaxpr/kgtu,ukd->kgtd/dot_general | solution.py:60
  162.0 1.1 constant_dynamic-slice_fusion.3
  163.2 3.7 %fusion.33 = (f32[2,5,384]{2,1,0:T(8,128)S(1)}, f32[2,384,384,5]{2,1,3,0:T(8,128)}) fusion(pred[384,384]{0,1:T(8,128)(4,1)S(1)} %or_and_fusion.2, bf16[384,2,128,1]{0,2,3,1:T(8,128)(2,1)S(1)} %bitcast.58, bf16[384,2,5,128]{3,0,2,1:T(8,128)(2,1)S(1)} %get-tuple-element.326), kind=kOutput, calls=%fused_computation.9.clone.1 | convolution fusion | flops 381907200 | bytes 7240704 | tf_op jit(solution)/shard_map/while/body/eval_jaxpr/tkgd,ukd->kgtu/dot_general | solution.py:42
  166.9 4.1 %fusion.34 = f32[2,5,384]{2,1,0:T(8,128)S(1)} fusion(f32[2,384,384,5]{2,1,3,0:T(8,128)} %get-tuple-element.280, f32[2,5,384]{2,1,0:T(8,128)S(1)} %select_maximum_fusion.2, pred[384,384]{0,1:T(8,128)(4,1)S(1)} %or_and_fusion.2), kind=kLoop, calls=%fused_computation.11.clone.1 | loop fusion | flops 7368960 | bytes 6076416 | tf_op jit(solution)/shard_map/while/body/eval_jaxpr/reduce_sum | solution.py:59
  171.2 6.8 %fusion.36 = f32[2,5,384,128]{3,2,1,0:T(8,128)} fusion(f32[2,5,384,128]{3,2,1,0:T(8,128)} %get-tuple-element.303, bf16[384,2,128,1]{0,2,3,1:T(8,128)(2,1)S(1)} %bitcast.60, f32[2,384,384,5]{2,1,3,0:T(8,128)} %get-tuple-element.280, f32[2,5,384]{2,1,0:T(8,128)S(1)} %select_maximum_fusion.2, pred[384,384]{0,1:T(8,128)(4,1)S(1)} %or_and_fusion.2, ...), kind=kOutput, calls=%fused_computation.15.clone.1 | convolution fusion | flops 386334720 | bytes 10205185 | tf_op jit(solution)/shard_map/while/body/eval_jaxpr/kgtu,ukd->kgtd/dot_general | solution.py:60
  179.7 1.1 constant_dynamic-slice_fusion.3
  180.9 3.7 %fusion.33 = (f32[2,5,384]{2,1,0:T(8,128)S(1)}, f32[2,384,384,5]{2,1,3,0:T(8,128)}) fusion(pred[384,384]{0,1:T(8,128)(4,1)S(1)} %or_and_fusion.2, bf16[384,2,128,1]{0,2,3,1:T(8,128)(2,1)S(1)} %bitcast.58, bf16[384,2,5,128]{3,0,2,1:T(8,128)(2,1)S(1)} %get-tuple-element.326), kind=kOutput, calls=%fused_computation.9.clone.1 | convolution fusion | flops 381907200 | bytes 7240704 | tf_op jit(solution)/shard_map/while/body/eval_jaxpr/tkgd,ukd->kgtu/dot_general | solution.py:42
  184.6 4.1 %fusion.34 = f32[2,5,384]{2,1,0:T(8,128)S(1)} fusion(f32[2,384,384,5]{2,1,3,0:T(8,128)} %get-tuple-element.280, f32[2,5,384]{2,1,0:T(8,128)S(1)} %select_maximum_fusion.2, pred[384,384]{0,1:T(8,128)(4,1)S(1)} %or_and_fusion.2), kind=kLoop, calls=%fused_computation.11.clone.1 | loop fusion | flops 7368960 | bytes 6076416 | tf_op jit(solution)/shard_map/while/body/eval_jaxpr/reduce_sum | solution.py:59
  188.9 6.8 %fusion.36 = f32[2,5,384,128]{3,2,1,0:T(8,128)} fusion(f32[2,5,384,128]{3,2,1,0:T(8,128)} %get-tuple-element.303, bf16[384,2,128,1]{0,2,3,1:T(8,128)(2,1)S(1)} %bitcast.60, f32[2,384,384,5]{2,1,3,0:T(8,128)} %get-tuple-element.280, f32[2,5,384]{2,1,0:T(8,128)S(1)} %select_maximum_fusion.2, pred[384,384]{0,1:T(8,128)(4,1)S(1)} %or_and_fusion.2, ...), kind=kOutput, calls=%fused_computation.15.clone.1 | convolution fusion | flops 386334720 | bytes 10205185 | tf_op jit(solution)/shard_map/while/body/eval_jaxpr/kgtu,ukd->kgtd/dot_general | solution.py:60
  197.3 1.1 constant_dynamic-slice_fusion.3
  198.6 3.7 %fusion.33 = (f32[2,5,384]{2,1,0:T(8,128)S(1)}, f32[2,384,384,5]{2,1,3,0:T(8,128)}) fusion(pred[384,384]{0,1:T(8,128)(4,1)S(1)} %or_and_fusion.2, bf16[384,2,128,1]{0,2,3,1:T(8,128)(2,1)S(1)} %bitcast.58, bf16[384,2,5,128]{3,0,2,1:T(8,128)(2,1)S(1)} %get-tuple-element.326), kind=kOutput, calls=%fused_computation.9.clone.1 | convolution fusion | flops 381907200 | bytes 7240704 | tf_op jit(solution)/shard_map/while/body/eval_jaxpr/tkgd,ukd->kgtu/dot_general | solution.py:42
  202.3 4.1 %fusion.34 = f32[2,5,384]{2,1,0:T(8,128)S(1)} fusion(f32[2,384,384,5]{2,1,3,0:T(8,128)} %get-tuple-element.280, f32[2,5,384]{2,1,0:T(8,128)S(1)} %select_maximum_fusion.2, pred[384,384]{0,1:T(8,128)(4,1)S(1)} %or_and_fusion.2), kind=kLoop, calls=%fused_computation.11.clone.1 | loop fusion | flops 7368960 | bytes 6076416 | tf_op jit(solution)/shard_map/while/body/eval_jaxpr/reduce_sum | solution.py:59
  206.6 6.8 %fusion.36 = f32[2,5,384,128]{3,2,1,0:T(8,128)} fusion(f32[2,5,384,128]{3,2,1,0:T(8,128)} %get-tuple-element.303, bf16[384,2,128,1]{0,2,3,1:T(8,128)(2,1)S(1)} %bitcast.60, f32[2,384,384,5]{2,1,3,0:T(8,128)} %get-tuple-element.280, f32[2,5,384]{2,1,0:T(8,128)S(1)} %select_maximum_fusion.2, pred[384,384]{0,1:T(8,128)(4,1)S(1)} %or_and_fusion.2, ...), kind=kOutput, calls=%fused_computation.15.clone.1 | convolution fusion | flops 386334720 | bytes 10205185 | tf_op jit(solution)/shard_map/while/body/eval_jaxpr/kgtu,ukd->kgtd/dot_general | solution.py:60
  215.0 1.1 constant_dynamic-slice_fusion.3
  216.2 3.7 %fusion.33 = (f32[2,5,384]{2,1,0:T(8,128)S(1)}, f32[2,384,384,5]{2,1,3,0:T(8,128)}) fusion(pred[384,384]{0,1:T(8,128)(4,1)S(1)} %or_and_fusion.2, bf16[384,2,128,1]{0,2,3,1:T(8,128)(2,1)S(1)} %bitcast.58, bf16[384,2,5,128]{3,0,2,1:T(8,128)(2,1)S(1)} %get-tuple-element.326), kind=kOutput, calls=%fused_computation.9.clone.1 | convolution fusion | flops 381907200 | bytes 7240704 | tf_op jit(solution)/shard_map/while/body/eval_jaxpr/tkgd,ukd->kgtu/dot_general | solution.py:42
  220.0 4.1 %fusion.34 = f32[2,5,384]{2,1,0:T(8,128)S(1)} fusion(f32[2,384,384,5]{2,1,3,0:T(8,128)} %get-tuple-element.280, f32[2,5,384]{2,1,0:T(8,128)S(1)} %select_maximum_fusion.2, pred[384,384]{0,1:T(8,128)(4,1)S(1)} %or_and_fusion.2), kind=kLoop, calls=%fused_computation.11.clone.1 | loop fusion | flops 7368960 | bytes 6076416 | tf_op jit(solution)/shard_map/while/body/eval_jaxpr/reduce_sum | solution.py:59
  224.3 6.8 %fusion.36 = f32[2,5,384,128]{3,2,1,0:T(8,128)} fusion(f32[2,5,384,128]{3,2,1,0:T(8,128)} %get-tuple-element.303, bf16[384,2,128,1]{0,2,3,1:T(8,128)(2,1)S(1)} %bitcast.60, f32[2,384,384,5]{2,1,3,0:T(8,128)} %get-tuple-element.280, f32[2,5,384]{2,1,0:T(8,128)S(1)} %select_maximum_fusion.2, pred[384,384]{0,1:T(8,128)(4,1)S(1)} %or_and_fusion.2, ...), kind=kOutput, calls=%fused_computation.15.clone.1 | convolution fusion | flops 386334720 | bytes 10205185 | tf_op jit(solution)/shard_map/while/body/eval_jaxpr/kgtu,ukd->kgtd/dot_general | solution.py:60
  231.1 2.1 fusion.13
  233.9 1.9 reshape.203
  236.0 1.9 scatter_fusion
  237.9 60.0 %all_to_all.23 = bf16[8,128,1280]{2,1,0:T(8,128)(2,1)S(1)} all-to-all(bf16[8,128,1280]{2,1,0:T(8,128)(2,1)S(1)} %scatter_fusion), channel_id=1, replica_groups=mesh['dp'=8,'ctx'=8,'head'=4] {'ctx'}, dimensions={0} | all-to-all | bytes 5242880 | tf_op jit(solution)/shard_map/all_to_all | solution.py:121
  297.9 2.9 copy.50
  300.9 11.0 %all-to-all-start.1 = ((bf16[8,128,1280]{2,0,1:T(8,128)(2,1)}), bf16[8,128,1280]{2,0,1:T(8,128)(2,1)S(1)}, u32[]{:S(2)}, u32[]{:S(2)}) async-start(bf16[8,128,1280]{2,0,1:T(8,128)(2,1)} %copy.50), calls=%async_computation.1 | async-start | bytes 5242880 | tf_op jit(solution)/shard_map/all_to_all | solution.py:120
  314.7 29.1 %all-to-all-done.1 = bf16[8,128,1280]{2,0,1:T(8,128)(2,1)S(1)} async-done(((bf16[8,128,1280]{2,0,1:T(8,128)(2,1)}), bf16[8,128,1280]{2,0,1:T(8,128)(2,1)S(1)}, u32[]{:S(2)}, u32[]{:S(2)}) %all-to-all-start.1) | async-done | bytes 2621472 | tf_op jit(solution)/shard_map/all_to_all | solution.py:120
  343.9 3.5 copy.52
  347.4 4.5 %all_to_all.20 = bf16[8,32,5120]{2,1,0:T(8,128)(2,1)S(1)} reshape(bf16[8,32,4,1280]{3,2,1,0:T(4,128)(2,1)} %copy.52) | data formatting | bytes 5242880 | tf_op jit(solution)/shard_map/all_to_all | solution.py:120
  351.9 1.6 gather_fusion
  353.5 2.3 broadcast_select_fusion
  (108 shorter events, 19.9 us)
Async XLA Ops:
  7.2 42.6 %all-gather.3.cloned.1.call-start = ((), (), s32[]{:S(2)}) async-start(), calls=%async_computation.2 | async-start | bytes 1769472 | tf_op jit(solution)/shard_map/all_gather | solution.py:72
  7.9 82.3 %all-gather.5.cloned.1.call-start = ((), (), s32[]{:S(2)}) async-start(), calls=%async_computation.3 | async-start | bytes 1769472 | tf_op jit(solution)/shard_map/all_gather | solution.py:73
  300.9 43.0 %all-to-all-start.1 = ((bf16[8,128,1280]{2,0,1:T(8,128)(2,1)}), bf16[8,128,1280]{2,0,1:T(8,128)(2,1)S(1)}, u32[]{:S(2)}, u32[]{:S(2)}) async-start(bf16[8,128,1280]{2,0,1:T(8,128)(2,1)} %copy.50), calls=%async_computation.1 | async-start | bytes 5242880 | tf_op jit(solution)/shard_map/all_to_all | solution.py:120
Sparse Core Ops, SparseCore 0:
  9.8 39.9 all-gather.2
  51.6 38.5 all-gather.4
where the time goes:
time: 364 us; the launch traced here: 363 us
  waiting for transfers between devices  104 us (29%)
  matrix products  83.5 us (23%)
  blocking collectives  60 us (16%)
  other arithmetic  42.6 us (12%)
  local copies, waits for them, and re-layouts  40.8 us (11%)
  between operations  14.8 us (4%)
  starting transfers between devices  11.1 us (3%)
  loops' own time  5.53 us (2%)
    all_to_all x1, blocking collectives, local(): lax.all_to_all(outgoing, 'ctx', split_axis=0, concat_axis=0, tiled=True)  60 us
    dot_general x8, matrix products, attend_block(): jnp.einsum('kgtu,ukd->kgtd', weights.astype(jnp.bfloat16), value_head_ten...  53.7 us
    all_gather x1, waiting for transfers between devices, local(): value_rows = lax.all_gather(values, 'ctx', axis=0, tiled=True)  40.4 us
    all_gather x1, waiting for transfers between devices, local(): key_rows = lax.all_gather(keys, 'ctx', axis=0, tiled=True)  33.4 us
    reduce_sum x8, other arithmetic, attend_block(): run_sum = run_sum * factor + jnp.sum(weights, axis=-1)  32.8 us
    dot_general x8, matrix products, attend_block(): jnp.einsum('tkgd,ukd->kgtu', query_head_tensor, key_head_tensor, preferre...  29.8 us
    all_to_all x1, waiting for transfers between devices, local(): lax.all_to_all(lax.all_to_all(outgoing, 'ctx', split_axis=0, concat_axis=...  29.1 us
    dynamic_slice x32, local copies, waits for them, and re-layouts, local(): lax.scan(scan_step, (start_max, start_sum, start_acc), stacked)  15.7 us
  transfers between devices with their start and end apart: 3, of which 3 were waited for; matrix products, arithmetic and copies ran while one was open for 3% of the time, Pallas kernels for 0%

commit v1 on v0

v1 whole, which is shorter than its diff:
```python
import functools
import math

import jax
import jax.numpy as jnp
from jax import lax
from jax.experimental import pallas as pl
from jax.experimental.pallas import tpu as pltpu
from jax.sharding import PartitionSpec as P

MESH = pl.DeviceIdType.MESH
D = 128
BLK = 128
NZ = 8
NH = 4
NB = 3
GROUP = 5
SUB = BLK // NH
NBLK = NZ * NB
PROMPT_BLOCKS = 6
BAND_BLOCKS = 8
ROWS = NB * SUB
WIDTH = GROUP * D
SCALE = 1.0 / math.sqrt(D)
LOG2E = 1.4426950408889634
NEG = -1e30


def kernel(
    order_ref, resp_ref, q_ref, k_ref, v_ref, out_ref, lse_ref,
    kvbuf, kseq, vseq, qbuf, obuf, bias, lse_seq, lse_send, lse_recv, inv_ref,
    kv_send, q_send, o_send, l_send, p_send,
    kv_recv, x_recv, c_recv, f_recv, q_recv, o_recv, l_recv,
):
    z = lax.axis_index("ctx")
    h = lax.axis_index("head")
    my_k = z // 2 + 4 * lax.rem(z, 2)
    my_src = my_k // 2

    barrier = pltpu.get_barrier_semaphore()
    for dz in range(NZ):
        for e in range(NH):
            if (dz, e) != (0, 0):
                pl.semaphore_signal(
                    barrier,
                    inc=1,
                    device_id={"ctx": lax.rem(z + dz, NZ), "head": lax.rem(h + e, NH)},
                    device_id_type=MESH,
                )
    pl.semaphore_wait(barrier, NZ * NH - 1)

    def send(src, dst, send_sem, recv_sem, tz, th):
        mine = (tz == z) & (th == h)

        @pl.when(mine)
        def _():
            pltpu.make_async_copy(src, dst, recv_sem).start()

        @pl.when(jnp.logical_not(mine))
        def _():
            pltpu.make_async_remote_copy(
                src, dst, send_sem, recv_sem, device_id={"ctx": tz, "head": th}, device_id_type=MESH
            ).start()

    def sent(src, dst, send_sem, recv_sem, tz, th):
        mine = (tz == z) & (th == h)

        @pl.when(jnp.logical_not(mine))
        def _():
            pltpu.make_async_remote_copy(
                src, dst, send_sem, recv_sem, device_id={"ctx": tz, "head": th}, device_id_type=MESH
            ).wait_send()

    def landed(ref, sem):
        pltpu.make_async_copy(ref, ref, sem).wait()

    mine_blocks = pl.ds(NB * z, NB)
    kv_moves, q_moves = [], []
    for kk in range(2):
        head = 2 * h + kk
        tz = lax.rem(2 * head, NZ) + head // 4
        for r in range(NH):
            rows = pl.ds(SUB * r, SUB)
            for w, ref in enumerate((k_ref, v_ref)):
                n = (kk * NH + r) * 2 + w
                kv_moves.append((
                    ref.at[:, rows, pl.ds(D * kk, D)], kvbuf.at[r, w, mine_blocks],
                    kv_send.at[n], kv_recv, tz, r,
                ))
            q_moves.append((
                q_ref.at[:, rows, pl.ds(WIDTH * kk, WIDTH)], qbuf.at[mine_blocks],
                q_send.at[kk * NH + r], q_recv, tz, r,
            ))
    for move in kv_moves:
        send(*move)
    for move in q_moves:
        send(*move)

    def find(p, c):
        found = jnp.int32(0)
        for j in range(NBLK):
            found = jnp.where(order_ref[j] == p, j, found)
        inv_ref[p] = found
        return c

    lax.fori_loop(0, NBLK, find, 0)

    lane = lax.broadcasted_iota(jnp.int32, (ROWS, D), 1)
    row = lax.broadcasted_iota(jnp.int32, (ROWS, D), 0)
    row_pos = (row // SUB) * BLK + lax.rem(row, SUB) + SUB * h

    def band_start(o):
        return jnp.where(o < 2, 0, jnp.maximum(PROMPT_BLOCKS, NB * o - 5))

    def masks(o, c):
        q_pos = row_pos + o * (NB * BLK)
        start = jnp.full((ROWS, D), PROMPT_BLOCKS * BLK, jnp.int32)
        end = jnp.int32(PROMPT_BLOCKS * BLK)
        for n in range(resp_ref.shape[0]):
            end = end + resp_ref[n]
            start = jnp.where(q_pos >= end, end, start)
        start = jnp.where(o < 2, 0, start)
        for b in range(BAND_BLOCKS):
            key_pos = lane + (band_start(o) + b) * BLK
            allowed = (key_pos >= start) & (key_pos <= q_pos)
            bias[o, :, pl.ds(b * BLK, BLK)] = jnp.where(allowed, 0.0, NEG)
        return c

    lax.fori_loop(0, NZ, masks, 0)

    own = kvbuf.at[h]
    landed(own, kv_recv)
    x_peer = lax.rem(h + 2, NH)
    c_peer = h + 1 - 2 * lax.rem(h, 2)
    far = kvbuf.at[x_peer]
    moves = [
        (own, own, p_send.at[0], x_recv, z, x_peer),
        (own, own, p_send.at[1], c_recv, z, c_peer),
        (far, far, p_send.at[2], f_recv, z, c_peer),
    ]

    def copy(src, dst, send_sem, recv_sem, tz, th):
        return pltpu.make_async_remote_copy(
            src, dst, send_sem, recv_sem, device_id={"ctx": tz, "head": th}, device_id_type=MESH
        )

    copy(*moves[0]).start()
    copy(*moves[1]).start()
    landed(far, x_recv)
    copy(*moves[2]).start()
    landed(own, c_recv)
    landed(own, f_recv)

    def build(p, c):
        j = inv_ref[p]
        for r in range(NH):
            at = pl.ds(pl.multiple_of(p * BLK + r * SUB, SUB), SUB)
            kseq[at, :] = kvbuf[r, 0, j]
            vseq[at, :] = kvbuf[r, 1, j]
        return c

    lax.fori_loop(0, NBLK, build, 0)
    landed(qbuf, q_recv)

    def attend(o, spans):
        idx = [inv_ref[NB * o + b] for b in range(NB)]
        tile = jnp.zeros((ROWS, D), jnp.float32)
        for g in range(GROUP):
            cols = pl.ds(g * D, D)
            q = jnp.concatenate([qbuf[j, :, cols] for j in idx], axis=0)
            scores = []
            for at, use_bias in spans:
                s = lax.dot_general(
                    q, kseq[at, :], (((1,), (1,)), ((), ())), preferred_element_type=jnp.float32
                )
                if use_bias:
                    s = s + bias[o, :, pl.ds(0, s.shape[1])]
                scores.append(s)
            top = functools.reduce(jnp.maximum, [jnp.max(s, axis=1, keepdims=True) for s in scores])
            total = jnp.zeros((ROWS, 1), jnp.float32)
            acc = jnp.zeros((ROWS, D), jnp.float32)
            for (at, _), s in zip(spans, scores):
                w = jnp.exp2((s - top) * (SCALE * LOG2E))
                total = total + jnp.sum(w, axis=1, keepdims=True)
                acc = acc + jnp.dot(
                    w.astype(jnp.bfloat16), vseq[at, :], preferred_element_type=jnp.float32
                )
            res = (acc / total).astype(jnp.bfloat16)
            for b in range(NB):
                obuf[o, b, :, cols] = res[b * SUB : (b + 1) * SUB]
            tile = jnp.where(lane == g, top * SCALE + jnp.log(total), tile)
        tile = jnp.concatenate([tile, jnp.zeros((D - ROWS, D), jnp.float32)], axis=0).T[:8]
        for b in range(NB):
            lse_seq[NB * o + b] = tile if b == 0 else pltpu.roll(tile, D - SUB * b, 1)

    out_cols = pl.ds(pl.multiple_of(my_k * WIDTH, D), WIDTH)

    def o_move(o):
        return (obuf.at[o], out_ref.at[:, :, out_cols], o_send.at[o], o_recv, o, h)

    def owner(t, c):
        half = (t + 1) // 2
        o = lax.rem(z + 4 + half * (1 - 2 * lax.rem(t, 2)), NZ)

        @pl.when(o < 2)
        def _():
            attend(o, [(pl.ds(0, PROMPT_BLOCKS * BLK), True)])

        @pl.when(o >= 2)
        def _():
            first = pl.multiple_of(band_start(o) * BLK, BLK)
            attend(o, [
                (pl.ds(0, PROMPT_BLOCKS * BLK), False),
                (pl.ds(first, BAND_BLOCKS * BLK), True),
            ])

        send(*o_move(o))
        return c

    lax.fori_loop(0, NZ, owner, 0)

    lane8 = lax.broadcasted_iota(jnp.int32, (8, D), 1)

    def l_move(s):
        return (lse_send.at[s], lse_recv.at[lax.rem(my_k, 2), h], l_send.at[s], l_recv, s, my_src)

    for s in range(NZ):
        tile = lse_seq[order_ref[NB * s]]
        for b in range(1, NB):
            tile = jnp.where(
                lane8 >= SUB * b, pltpu.roll(lse_seq[order_ref[NB * s + b]], SUB * b, 1), tile
            )
        lse_send[s] = tile
        send(*l_move(s))

    landed(lse_recv, l_recv)
    for kk in range(2):
        for b in range(NB):
            tile = jnp.zeros((8, D), jnp.float32)
            for r in range(NH):
                shift = (SUB * (r - b)) % D
                part = lse_recv[kk, r]
                part = pltpu.roll(part, shift, 1) if shift else part
                tile = jnp.where(lane8 >= SUB * r, part, tile)
            lse_ref[pl.ds(kk * GROUP, GROUP), pl.ds(b * BLK, BLK)] = tile[:GROUP]

    for move in kv_moves + q_moves:
        sent(*move)
    for move in moves:
        copy(*move).wait_send()
    for s in range(NZ):
        sent(*o_move(jnp.int32(s)))
        sent(*l_move(jnp.int32(s)))
    landed(out_ref, o_recv)


def solution(mesh):
    def step(q, k, v, order, resp):
        q = q.reshape(NB, BLK, q.shape[1])
        k = k.reshape(NB, BLK, k.shape[1])
        v = v.reshape(NB, BLK, v.shape[1])
        smem = pl.BlockSpec(memory_space=pltpu.SMEM)
        hbm = pl.BlockSpec(memory_space=pl.ANY)
        vmem = pl.BlockSpec(memory_space=pltpu.VMEM)
        dma = pltpu.SemaphoreType.DMA
        return pl.pallas_call(
            kernel,
            out_shape=(
                jax.ShapeDtypeStruct((NB, SUB, NZ * WIDTH), jnp.bfloat16),
                jax.ShapeDtypeStruct((2 * GROUP, NB * BLK), jnp.float32),
            ),
            in_specs=[smem, smem, hbm, hbm, hbm],
            out_specs=(vmem, vmem),
            scratch_shapes=[
                pltpu.VMEM((NH, 2, NBLK, SUB, D), jnp.bfloat16),
                pltpu.VMEM((NBLK * BLK, D), jnp.bfloat16),
                pltpu.VMEM((NBLK * BLK, D), jnp.bfloat16),
                pltpu.VMEM((NBLK, SUB, WIDTH), jnp.bfloat16),
                pltpu.VMEM((NZ, NB, SUB, WIDTH), jnp.bfloat16),
                pltpu.VMEM((NZ, ROWS, BAND_BLOCKS * BLK), jnp.float32),
                pltpu.VMEM((NBLK, 8, D), jnp.float32),
                pltpu.VMEM((NZ, 8, D), jnp.float32),
                pltpu.VMEM((2, NH, 8, D), jnp.float32),
                pltpu.SMEM((NBLK,), jnp.int32),
                dma((4 * NH,)), dma((2 * NH,)), dma((NZ,)), dma((NZ,)), dma((3,)),
                dma, dma, dma, dma, dma, dma, dma,
            ],
            compiler_params=pltpu.CompilerParams(
                collective_id=0, has_side_effects=True, vmem_limit_bytes=44 << 20
            ),
        )(order, resp, q, k, v)

    rows = P(("dp", "ctx"), "head")
    return jax.shard_map(
        step,
        mesh=mesh,
        in_specs=(rows, rows, rows, P("dp"), P("dp")),
        out_specs=(P(("dp", "ctx"), "head", None), P("head", ("dp", "ctx"))),
        check_vma=False,
    )
```

time: 364 us -> 92.6 us (0.25)
  waiting for transfers between devices: 104 us -> 0 us
  Pallas kernels: 0 us -> 86.5 us
  matrix products: 83.5 us -> 0 us
  blocking collectives: 60 us -> 0 us
  other arithmetic: 42.6 us -> 0 us
  local copies, waits for them, and re-layouts: 40.8 us -> 5.26 us
  between operations: 14.8 us -> 0.66 us
  starting transfers between devices: 11.1 us -> 0 us
  loops' own time: 5.53 us -> 0 us
    pallas_call x0 -> x1, Pallas kernels: none -> 86.5 us  [step(): pl.pallas_call(kernel, out_shape=(jax.ShapeDtypeStruct((NB, SUB, NZ * WID...]
    dot_general x16 -> x0, matrix products: 83.5 us -> none  [the longest x8 53.7 us: attend_block(): jnp.einsum('kgtu,ukd->kgtd', weights.astype(jnp.bfloat16), value_head_ten...]
    all_gather x2 -> x0, waiting for transfers between devices: 73.8 us -> none  [the longest x1 40.4 us: local(): value_rows = lax.all_gather(values, 'ctx', axis=0, tiled=True)]
    all_to_all x1 -> x0, blocking collectives: 60 us -> none  [local(): lax.all_to_all(outgoing, 'ctx', split_axis=0, concat_axis=0, tiled=True)]
    reduce_sum x11 -> x0, other arithmetic: 34.4 us -> none  [the longest x8 32.8 us: attend_block(): run_sum = run_sum * factor + jnp.sum(weights, axis=-1)]
    all_to_all x1 -> x0, waiting for transfers between devices: 29.1 us -> none  [local(): lax.all_to_all(lax.all_to_all(outgoing, 'ctx', split_axis=0, concat_axis=...]
    dynamic_slice x42 -> x0, local copies, waits for them, and re-layouts: 16.5 us -> none  [the longest x32 15.7 us: local(): lax.scan(scan_step, (start_max, start_sum, start_acc), stacked)]
    all_to_all x1 -> x0, starting transfers between devices: 11 us -> none  [local(): lax.all_to_all(lax.all_to_all(outgoing, 'ctx', split_axis=0, concat_axis=...]
  transfers between devices with their start and end apart: 3 -> 0, of which waited for: 3 -> 0; matrix products, arithmetic and copies ran while one was open for 3% -> 0% of each run, Pallas kernels for 0% -> 0%
where the time goes in v1:
time: 92.6 us; the launch traced here: 92.4 us
  Pallas kernels  86.5 us (93%)
  local copies, waits for them, and re-layouts  5.26 us (6%)
    pallas_call x1, Pallas kernels, step(): pl.pallas_call(kernel, out_shape=(jax.ShapeDtypeStruct((NB, SUB, NZ * WID...  86.5 us
    unnamed x12, local copies, waits for them, and re-layouts  5.26 us

profile of v1, /device:TPU:1, one launch (start us, length us, event | category | flops | bytes accessed | tf_op | source)
XLA Modules:
  0.0 92.4 jit_solution(2492705164448867335)
XLA Ops:
  0.6 0.0 copy-start.3
  0.6 0.0 copy-start.4
  0.7 0.6 copy-done.3
  1.3 0.0 copy-done.4
  1.3 0.0 copy-start
  1.3 1.2 %copy-done = bf16[384,1280]{1,0:T(8,128)(2,1)S(1)} copy-done((bf16[384,1280]{1,0:T(8,128)(2,1)S(1)}, bf16[384,1280]{1,0:T(8,128)(2,1)}, u32[]{:S(2)}) %copy-start) | copy-done | bytes 983064
  2.5 0.0 copy-start.1
  2.5 0.9 %copy-done.1 = bf16[384,256]{1,0:T(8,128)(2,1)S(1)} copy-done((bf16[384,256]{1,0:T(8,128)(2,1)S(1)}, bf16[384,256]{1,0:T(8,128)(2,1)}, u32[]{:S(2)}) %copy-start.1) | copy-done | bytes 196632
  3.4 0.0 copy-start.2
  3.4 0.9 %copy-done.2 = bf16[384,256]{1,0:T(8,128)(2,1)S(1)} copy-done((bf16[384,256]{1,0:T(8,128)(2,1)S(1)}, bf16[384,256]{1,0:T(8,128)(2,1)}, u32[]{:S(2)}) %copy-start.2) | copy-done | bytes 196632
  4.4 86.5 %shard_map.68 = (bf16[3,32,5120]{2,1,0:T(8,128)(2,1)S(1)}, f32[10,384]{1,0:T(8,128)S(1)}) custom-call(s32[24]{0:T(128)S(1)} %copy-done.3, s32[16]{0:T(128)S(1)} %copy-done.4, bf16[3,128,1280]{2,1,0:T(8,128)(2,1)S(1)} %bitcast.3, bf16[3,128,256]{2,1,0:T(8,128)(2,1)S(1)} %bitcast.4, bf16[3,128,256]{2,1,0:T(8,128)(2,1)S(1)} %bitcast.5), custom_call_target="tpu_custom_call" | custom-call | tf_op jit(solution)/shard_map/pallas_call | solution.py:266
  90.9 0.9 %copy.9 = bf16[3,32,5120]{2,1,0:T(8,128)(2,1)} copy(bf16[3,32,5120]{2,1,0:T(8,128)(2,1)S(1)} %get-tuple-element.4) | data formatting | bytes 1966080
  91.8 0.6 copy.10
Async XLA Ops:
  0.6 0.7 copy-start.3
  0.6 0.7 copy-start.4
  1.3 1.2 %copy-start = (bf16[384,1280]{1,0:T(8,128)(2,1)S(1)}, bf16[384,1280]{1,0:T(8,128)(2,1)}, u32[]{:S(2)}) copy-start(bf16[384,1280]{1,0:T(8,128)(2,1)} %param.5) | copy-start | bytes 2949124
  2.5 0.9 %copy-start.1 = (bf16[384,256]{1,0:T(8,128)(2,1)S(1)}, bf16[384,256]{1,0:T(8,128)(2,1)}, u32[]{:S(2)}) copy-start(bf16[384,256]{1,0:T(8,128)(2,1)} %param.6) | copy-start | bytes 589828
  3.4 0.9 %copy-start.2 = (bf16[384,256]{1,0:T(8,128)(2,1)S(1)}, bf16[384,256]{1,0:T(8,128)(2,1)}, u32[]{:S(2)}) copy-start(bf16[384,256]{1,0:T(8,128)(2,1)} %param.7) | copy-start | bytes 589828

commit v2 on v1

v2 whole, which is shorter than its diff:
```python
import functools
import math

import jax
import jax.numpy as jnp
from jax import lax
from jax.experimental import pallas as pl
from jax.experimental.pallas import tpu as pltpu
from jax.sharding import PartitionSpec as P

MESH = pl.DeviceIdType.MESH
D = 128
BLK = 128
NZ = 8
NH = 4
NB = 3
GROUP = 5
SUB = BLK // NH
NBLK = NZ * NB
PROMPT_BLOCKS = 6
BAND_BLOCKS = 8
ROWS = NB * SUB
WIDTH = GROUP * D
CHUNKS = ((0, 3), (3, 5))
SCALE = 1.0 / math.sqrt(D)
LOG2E = 1.4426950408889634
NEG = -1e30


def kernel(
    order_ref, resp_ref, q_ref, k_ref, v_ref, out_ref, lse_ref,
    vstage, qstage, kv, kseq, vseq, qbuf_a, qbuf_b, obuf_a, obuf_b, bias,
    lse_seq, lse_send, lse_z, lse_recv, inv_ref,
    kv_send, v_send, q1_send, q2_send, x_send, c_send, o_send, l_send, l2_send,
    v_recv, q1_recv, q2_recv, z_recv, x_recv, c_recv, o_recv, l_recv, l2_recv,
):
    z = lax.axis_index("ctx")
    h = lax.axis_index("head")
    x_peer = lax.rem(h + 2, NH)
    c_peer = h + 1 - 2 * lax.rem(h, 2)
    d_peer = lax.rem(c_peer + 2, NH)
    my_k = z // 2 + 4 * lax.rem(z, 2)
    my_src = my_k // 2
    qbuf, obuf = (qbuf_a, qbuf_b), (obuf_a, obuf_b)

    barrier = pltpu.get_barrier_semaphore()
    for dz in range(1, NZ):
        pl.semaphore_signal(
            barrier, inc=1, device_id={"ctx": lax.rem(z + dz, NZ)}, device_id_type=MESH
        )
    for th in (c_peer, x_peer, d_peer):
        pl.semaphore_signal(barrier, inc=1, device_id={"head": th}, device_id_type=MESH)
    pl.semaphore_wait(barrier, NZ - 1 + NH - 1)

    def plane(k):
        return lax.rem(2 * k, NZ) + k // 4

    def remote(src, dst, send_sem, recv_sem, tz, th):
        return pltpu.make_async_remote_copy(
            src, dst, send_sem, recv_sem, device_id={"ctx": tz, "head": th}, device_id_type=MESH
        )

    def send(src, dst, send_sem, recv_sem, tz):
        @pl.when(tz == z)
        def _():
            pltpu.make_async_copy(src, dst, recv_sem).start()

        @pl.when(tz != z)
        def _():
            remote(src, dst, send_sem, recv_sem, tz, h).start()

    def sent(src, dst, send_sem, recv_sem, tz):
        @pl.when(tz != z)
        def _():
            remote(src, dst, send_sem, recv_sem, tz, h).wait_send()

    def landed(ref, sem):
        pltpu.make_async_copy(ref, ref, sem).wait()

    here = pl.ds(NB * z, NB)

    k_moves = [
        (k_ref.at[:, :, pl.ds(D * kk, D)], kv.at[0, here], kv_send.at[kk], z_recv.at[z],
         plane(2 * h + kk))
        for kk in range(2)
    ]
    v_moves = [
        (vstage.at[:, :, pl.ds(D * kk, D)], kv.at[1, here], kv_send.at[2 + kk], z_recv.at[z],
         plane(2 * x_peer + kk))
        for kk in range(2)
    ]
    v_move = (v_ref, vstage, v_send, v_recv, z, x_peer)
    remote(*v_move).start()
    for move in k_moves:
        send(*move)

    def q_cols(c, kk):
        first, last = CHUNKS[c]
        return pl.ds(WIDTH * kk + D * first, D * (last - first))

    q1_moves = []
    for c in range(2):
        for kk in range(2):
            cols = q_cols(c, kk)
            dst = qstage.at[h, :, :, cols]
            n = 2 * c + kk
            pltpu.make_async_copy(
                q_ref.at[:, pl.ds(pl.multiple_of(SUB * h, SUB), SUB), cols], dst, q1_recv.at[n, h]
            ).start()
            for e, th in enumerate((c_peer, x_peer, d_peer)):
                rows = pl.ds(pl.multiple_of(SUB * th, SUB), SUB)
                move = (q_ref.at[:, rows, cols], dst, q1_send.at[n, e], q1_recv.at[n, h], z, th)
                remote(*move).start()
                q1_moves.append(move)

    q2_moves = []

    def forward(c):
        for e, hd in enumerate((h, c_peer, x_peer, d_peer)):
            for kk in range(2):
                src = qstage.at[hd, :, :, q_cols(c, kk)]
                move = (
                    src, qbuf[c].at[here], q2_send.at[c, 2 * e + kk], q2_recv.at[c],
                    plane(2 * hd + kk),
                )
                landed(src, q1_recv.at[2 * c + kk, hd])
                send(*move)
                q2_moves.append(move)

    landed(vstage, v_recv)
    for move in v_moves:
        send(*move)
    forward(0)

    primary = lax.rem(h, 2) == lax.rem(my_src, 2)
    which = lax.rem(h // 2 + my_src // 2, 2)

    def piece(w, s):
        return kv.at[w, pl.ds(NB * s, NB)]

    def x_move(s):
        src = piece(which, s)
        return (src, src, x_send.at[s], x_recv.at[s], z, x_peer)

    def c_move(w, s):
        src = piece(w, s)
        return (src, src, c_send.at[w, s], c_recv, z, c_peer)

    def source(t):
        return lax.rem(z + 4 + ((t + 1) // 2) * (1 - 2 * lax.rem(t, 2)), NZ)

    @pl.when(primary)
    def _():
        def own(t, c):
            s = source(NZ - 1 - t)
            landed(piece(which, s), z_recv.at[s])
            remote(*x_move(s)).start()
            remote(*c_move(which, s)).start()
            return c

        lax.fori_loop(0, NZ, own, 0)

    forward(1)

    def find(p, c):
        found = jnp.int32(0)
        for j in range(NBLK):
            found = jnp.where(order_ref[j] == p, j, found)
        inv_ref[p] = found
        return c

    lax.fori_loop(0, NBLK, find, 0)

    lane = lax.broadcasted_iota(jnp.int32, (ROWS, D), 1)
    row = lax.broadcasted_iota(jnp.int32, (ROWS, D), 0)
    row_pos = (row // SUB) * BLK + lax.rem(row, SUB) + SUB * h

    def band_start(o):
        return jnp.where(o < 2, 0, jnp.maximum(PROMPT_BLOCKS, NB * o - 5))

    def masks(o, c):
        q_pos = row_pos + o * (NB * BLK)
        start = jnp.full((ROWS, D), PROMPT_BLOCKS * BLK, jnp.int32)
        end = jnp.int32(PROMPT_BLOCKS * BLK)
        for n in range(resp_ref.shape[0]):
            end = end + resp_ref[n]
            start = jnp.where(q_pos >= end, end, start)
        start = jnp.where(o < 2, 0, start)
        for b in range(BAND_BLOCKS):
            key_pos = lane + (band_start(o) + b) * BLK
            allowed = (key_pos >= start) & (key_pos <= q_pos)
            bias[o, :, pl.ds(b * BLK, BLK)] = jnp.where(allowed, 0.0, NEG)
        return c

    lax.fori_loop(0, NZ, masks, 0)

    @pl.when(primary)
    def _():
        def other(t, c):
            s = source(NZ - 1 - t)
            landed(piece(1 - which, s), x_recv.at[s])
            remote(*c_move(1 - which, s)).start()
            return c

        lax.fori_loop(0, NZ, other, 0)

    @pl.when(jnp.logical_not(primary))
    def _():
        landed(kv, c_recv)

    def build(p, c):
        j = inv_ref[p]
        at = pl.ds(pl.multiple_of(p * BLK, BLK), BLK)
        kseq[at, :] = kv[0, j]
        vseq[at, :] = kv[1, j]
        return c

    lax.fori_loop(0, NBLK, build, 0)

    def attend(c, o, spans):
        idx = [inv_ref[NB * o + b] for b in range(NB)]
        tile = jnp.zeros((ROWS, D), jnp.float32)
        for g in range(*CHUNKS[c]):
            cols = pl.ds((g - CHUNKS[c][0]) * D, D)
            q = jnp.concatenate([qbuf[c][j, :, cols] for j in idx], axis=0)
            scores = []
            for at, use_bias in spans:
                s = lax.dot_general(
                    q, kseq[at, :], (((1,), (1,)), ((), ())), preferred_element_type=jnp.float32
                )
                if use_bias:
                    s = s + bias[o, :, pl.ds(0, s.shape[1])]
                scores.append(s)
            top = functools.reduce(jnp.maximum, [jnp.max(s, axis=1, keepdims=True) for s in scores])
            total = jnp.zeros((ROWS, 1), jnp.float32)
            acc = jnp.zeros((ROWS, D), jnp.float32)
            for (at, _), s in zip(spans, scores):
                w = jnp.exp2((s - top) * (SCALE * LOG2E))
                total = total + jnp.sum(w, axis=1, keepdims=True)
                acc = acc + jnp.dot(
                    w.astype(jnp.bfloat16), vseq[at, :], preferred_element_type=jnp.float32
                )
            res = (acc / total).astype(jnp.bfloat16)
            for b in range(NB):
                obuf[c][o, b, :, cols] = res[b * SUB : (b + 1) * SUB]
            tile = jnp.where(lane == g, top * SCALE + jnp.log(total), tile)
        tile = jnp.concatenate([tile, jnp.zeros((D - ROWS, D), jnp.float32)], axis=0).T[:8]
        for b in range(NB):
            part = tile if b == 0 else pltpu.roll(tile, D - SUB * b, 1)
            lse_seq[NB * o + b] = part if c == 0 else part + lse_seq[NB * o + b]

    def o_move(c, o):
        first, last = CHUNKS[c]
        cols = pl.ds(pl.multiple_of(my_k * WIDTH + first * D, D), (last - first) * D)
        return (obuf[c].at[o], out_ref.at[:, :, cols], o_send.at[c, o], o_recv, o)

    for c in range(2):
        landed(qbuf[c], q2_recv.at[c])

        def owner(t, carry, c=c):
            o = source(t)

            @pl.when(o < 2)
            def _():
                attend(c, o, [(pl.ds(0, PROMPT_BLOCKS * BLK), True)])

            @pl.when(o >= 2)
            def _():
                first = pl.multiple_of(band_start(o) * BLK, BLK)
                attend(c, o, [
                    (pl.ds(0, PROMPT_BLOCKS * BLK), False),
                    (pl.ds(first, BAND_BLOCKS * BLK), True),
                ])

            send(*o_move(c, o))
            return carry

        lax.fori_loop(0, NZ, owner, 0)

    lane8 = lax.broadcasted_iota(jnp.int32, (8, D), 1)

    def l_move(s):
        return (lse_send.at[s], lse_z.at[my_k], l_send.at[s], l_recv, s)

    def l2_move(e, th):
        return (lse_z.at[pl.ds(2 * th, 2)], lse_recv.at[h], l2_send.at[e], l2_recv, z, th)

    for s in range(NZ):
        tile = lse_seq[order_ref[NB * s]]
        for b in range(1, NB):
            tile = jnp.where(
                lane8 >= SUB * b, pltpu.roll(lse_seq[order_ref[NB * s + b]], SUB * b, 1), tile
            )
        lse_send[s] = tile
        send(*l_move(s))

    landed(lse_z, l_recv)
    pltpu.make_async_copy(lse_z.at[pl.ds(2 * h, 2)], lse_recv.at[h], l2_recv).start()
    for e, th in enumerate((c_peer, x_peer, d_peer)):
        remote(*l2_move(e, th)).start()
    landed(lse_recv, l2_recv)
    for kk in range(2):
        for b in range(NB):
            tile = jnp.zeros((8, D), jnp.float32)
            for r in range(NH):
                shift = (SUB * (r - b)) % D
                part = lse_recv[r, kk]
                part = pltpu.roll(part, shift, 1) if shift else part
                tile = jnp.where(lane8 >= SUB * r, part, tile)
            lse_ref[pl.ds(kk * GROUP, GROUP), pl.ds(b * BLK, BLK)] = tile[:GROUP]

    remote(*v_move).wait_send()
    for move in k_moves + v_moves + q2_moves:
        sent(*move)
    for move in q1_moves:
        remote(*move).wait_send()
    for e, th in enumerate((c_peer, x_peer, d_peer)):
        remote(*l2_move(e, th)).wait_send()

    @pl.when(primary)
    def _():
        def done(s, c):
            remote(*x_move(s)).wait_send()
            remote(*c_move(0, s)).wait_send()
            remote(*c_move(1, s)).wait_send()
            return c

        lax.fori_loop(0, NZ, done, 0)

    for s in range(NZ):
        sent(*l_move(jnp.int32(s)))
        for c in range(2):
            sent(*o_move(c, jnp.int32(s)))
    landed(out_ref, o_recv)


def solution(mesh):
    def step(q, k, v, order, resp):
        q = q.reshape(NB, BLK, q.shape[1])
        k = k.reshape(NB, BLK, k.shape[1])
        v = v.reshape(NB, BLK, v.shape[1])
        smem = pl.BlockSpec(memory_space=pltpu.SMEM)
        hbm = pl.BlockSpec(memory_space=pl.ANY)
        vmem = pl.BlockSpec(memory_space=pltpu.VMEM)
        dma = pltpu.SemaphoreType.DMA
        bf16 = lambda *shape: pltpu.VMEM(shape, jnp.bfloat16)
        f32 = lambda *shape: pltpu.VMEM(shape, jnp.float32)
        widths = [D * (last - first) for first, last in CHUNKS]
        return pl.pallas_call(
            kernel,
            out_shape=(
                jax.ShapeDtypeStruct((NB, SUB, NZ * WIDTH), jnp.bfloat16),
                jax.ShapeDtypeStruct((2 * GROUP, NB * BLK), jnp.float32),
            ),
            in_specs=[smem, smem, hbm, hbm, hbm],
            out_specs=(vmem, vmem),
            scratch_shapes=[
                bf16(NB, BLK, 2 * D),
                bf16(NH, NB, SUB, 2 * WIDTH),
                bf16(2, NBLK, BLK, D),
                bf16(NBLK * BLK, D),
                bf16(NBLK * BLK, D),
                *[bf16(NBLK, SUB, w) for w in widths],
                *[bf16(NZ, NB, SUB, w) for w in widths],
                f32(NZ, ROWS, BAND_BLOCKS * BLK),
                f32(NBLK, 8, D),
                f32(NZ, 8, D),
                f32(NZ, 8, D),
                f32(NH, 2, 8, D),
                pltpu.SMEM((NBLK,), jnp.int32),
                dma((4,)), dma, dma((4, NH - 1)), dma((2, NZ)), dma((NZ,)), dma((2, NZ)),
                dma((2, NZ)), dma((NZ,)), dma((NH - 1,)),
                dma, dma((4, NH)), dma((2,)), dma((NZ,)), dma((NZ,)), dma, dma, dma, dma,
            ],
            compiler_params=pltpu.CompilerParams(
                collective_id=0, has_side_effects=True, vmem_limit_bytes=60 << 20
            ),
        )(order, resp, q, k, v)

    rows = P(("dp", "ctx"), "head")
    return jax.shard_map(
        step,
        mesh=mesh,
        in_specs=(rows, rows, rows, P("dp"), P("dp")),
        out_specs=(P(("dp", "ctx"), "head", None), P("head", ("dp", "ctx"))),
        check_vma=False,
    )
```

time: 92.6 us -> 85.6 us (0.924)
  Pallas kernels: 86.5 us -> 82.1 us
  local copies, waits for them, and re-layouts: 5.26 us -> 2.83 us
    pallas_call x1, Pallas kernels: 86.5 us -> 82.1 us  [step(): pl.pallas_call(kernel, out_shape=(jax.ShapeDtypeStruct((NB, SUB, NZ * WID...]
    unnamed x12 -> x4, local copies, waits for them, and re-layouts: 5.26 us -> 2.83 us
where the time goes in v2:
time: 85.6 us; the launch traced here: 85.5 us
  Pallas kernels  82.1 us (96%)
  local copies, waits for them, and re-layouts  2.83 us (3%)
    pallas_call x1, Pallas kernels, step(): pl.pallas_call(kernel, out_shape=(jax.ShapeDtypeStruct((NB, SUB, NZ * WID...  82.1 us
    unnamed x4, local copies, waits for them, and re-layouts  2.83 us

profile of v2, /device:TPU:1, one launch (start us, length us, event | category | flops | bytes accessed | tf_op | source)
XLA Modules:
  0.0 85.5 jit_solution(7110246983507910036)
XLA Ops:
  0.6 82.1 %shard_map.68 = (bf16[3,32,5120]{2,1,0:T(8,128)(2,1)}, f32[10,384]{1,0:T(8,128)}) custom-call(s32[24]{0:T(128)} %order_ref.1, s32[16]{0:T(128)} %resp_ref.1, bf16[3,128,1280]{2,1,0:T(8,128)(2,1)} %bitcast.3, bf16[3,128,256]{2,1,0:T(8,128)(2,1)} %bitcast.4, bf16[3,128,256]{2,1,0:T(8,128)(2,1)} %bitcast.5), custom_call_target="tpu_custom_call" | custom-call | tf_op jit(solution)/shard_map/pallas_call | solution.py:349
  82.7 0.0 copy-start
  82.7 2.2 %copy.9 = bf16[3,32,5120]{2,1,0:T(8,128)(2,1)} copy(bf16[3,32,5120]{2,1,0:T(8,128)(2,1)} %get-tuple-element.4) | data formatting | bytes 1966080
  84.9 0.0 copy-done
  84.9 0.6 copy.10
Async XLA Ops:
  82.7 2.2 %copy-start = (f32[10,384]{1,0:T(8,128)S(1)}, f32[10,384]{1,0:T(8,128)}, u32[]{:S(2)}) copy-start(f32[10,384]{1,0:T(8,128)} %get-tuple-element.5) | copy-start | bytes 46084

commit v3 on v2

v3 whole, which is shorter than its diff:
```python
import functools
import math

import jax
import jax.numpy as jnp
from jax import lax
from jax.experimental import pallas as pl
from jax.experimental.pallas import tpu as pltpu
from jax.sharding import PartitionSpec as P

MESH = pl.DeviceIdType.MESH
D = 128
BLK = 128
NZ = 8
NH = 4
NB = 3
GROUP = 5
SUB = BLK // NH
NBLK = NZ * NB
PROMPT_BLOCKS = 6
BAND_BLOCKS = 8
ROWS = NB * SUB
WIDTH = GROUP * D
CHUNKS = ((0, 3), (3, 5))
SCALE = 1.0 / math.sqrt(D)
LOG2E = 1.4426950408889634
NEG = -1e30
HELD = 5


def kernel(
    order_ref, resp_ref, q_ref, k_ref, v_ref, out_ref, lse_ref,
    vstage, qstage, kv, kseq, vseq, qbuf, obuf, bias,
    lse_seq, lse_send, lse_recv, inv_ref,
    kv_send, v_send, q1_send, q2_send, x_send, c_send, o_send, l_send,
    v_recv, q1_recv, q2_recv, z_recv, x_recv, c_recv, o_recv, l_recv,
):
    z = lax.axis_index("ctx")
    h = lax.axis_index("head")
    x_peer = lax.rem(h + 2, NH)
    c_peer = h + 1 - 2 * lax.rem(h, 2)
    d_peer = lax.rem(c_peer + 2, NH)
    peers = (c_peer, x_peer, d_peer)

    def plane(k):
        return lax.rem(2 * k, NZ) + k // 4

    my_k = z // 2 + 4 * lax.rem(z, 2)
    my_src = my_k // 2

    barrier = pltpu.get_barrier_semaphore()
    for dz in range(1, NZ):
        pl.semaphore_signal(
            barrier, inc=1, device_id={"ctx": lax.rem(z + dz, NZ)}, device_id_type=MESH
        )
    for th in peers:
        pl.semaphore_signal(barrier, inc=1, device_id={"head": th}, device_id_type=MESH)
    for kk in range(2):
        tz = plane(2 * h + kk)

        @pl.when(tz != z)
        def _():
            for th in peers:
                pl.semaphore_signal(
                    barrier, inc=1, device_id={"ctx": tz, "head": th}, device_id_type=MESH
                )

    pl.semaphore_wait(barrier, NZ - 1 + NH - 1 + jnp.where(my_src == h, 0, NZ - 1))

    def remote(src, dst, send_sem, recv_sem, tz, th):
        return pltpu.make_async_remote_copy(
            src, dst, send_sem, recv_sem, device_id={"ctx": tz, "head": th}, device_id_type=MESH
        )

    def send(src, dst, send_sem, recv_sem, tz, th=h):
        mine = (tz == z) & (th == h)

        @pl.when(mine)
        def _():
            pltpu.make_async_copy(src, dst, recv_sem).start()

        @pl.when(jnp.logical_not(mine))
        def _():
            remote(src, dst, send_sem, recv_sem, tz, th).start()

    def sent(src, dst, send_sem, recv_sem, tz, th=h):
        @pl.when(jnp.logical_not((tz == z) & (th == h)))
        def _():
            remote(src, dst, send_sem, recv_sem, tz, th).wait_send()

    def landed(ref, sem):
        pltpu.make_async_copy(ref, ref, sem).wait()

    here = pl.ds(NB * z, NB)

    k_moves = [
        (k_ref.at[:, :, pl.ds(D * kk, D)], kv.at[0, here], kv_send.at[kk], z_recv.at[z],
         plane(2 * h + kk))
        for kk in range(2)
    ]
    v_moves = [
        (vstage.at[:, :, pl.ds(D * kk, D)], kv.at[1, here], kv_send.at[2 + kk], z_recv.at[z],
         plane(2 * x_peer + kk))
        for kk in range(2)
    ]
    v_move = (v_ref, vstage, v_send, v_recv, z, x_peer)
    remote(*v_move).start()
    for move in k_moves:
        send(*move)

    def q_cols(kk):
        return pl.ds(WIDTH * kk, WIDTH)

    def q1_move(e, kk):
        rows = pl.ds(pl.multiple_of(SUB * peers[e], SUB), SUB)
        return (
            q_ref.at[:, rows, q_cols(kk)], qstage.at[h, :, :, q_cols(kk)],
            q1_send.at[kk, e], q1_recv.at[kk, h], z, peers[e],
        )

    q1_moves = [q1_move(e, kk) for e in range(NH - 1) for kk in range(2)]
    for move in q1_moves[:2]:
        remote(*move).start()

    def q2_move(e, hd, kk):
        if e == 0:
            src = q_ref.at[:, pl.ds(pl.multiple_of(SUB * h, SUB), SUB), q_cols(kk)]
        else:
            src = qstage.at[hd, :, :, q_cols(kk)]
        return (src, qbuf.at[here], q2_send.at[e, kk], q2_recv, plane(2 * hd + kk))

    q2_moves = []

    def forward(e):
        hd = (h, *peers)[e]
        for kk in range(2):
            move = q2_move(e, hd, kk)
            if e:
                landed(move[0], q1_recv.at[kk, hd])
            send(*move)
            q2_moves.append(move)

    def find(p, c):
        found = jnp.int32(0)
        for j in range(NBLK):
            found = jnp.where(order_ref[j] == p, j, found)
        inv_ref[p] = found
        return c

    lax.fori_loop(0, NBLK, find, 0)

    lane = lax.broadcasted_iota(jnp.int32, (ROWS, D), 1)
    row = lax.broadcasted_iota(jnp.int32, (ROWS, D), 0)
    row_pos = (row // SUB) * BLK + lax.rem(row, SUB) + SUB * h

    def band_start(o):
        return jnp.where(o < 2, 0, jnp.maximum(PROMPT_BLOCKS, NB * o - 5))

    def masks(o, c):
        q_pos = row_pos + o * (NB * BLK)
        start = jnp.full((ROWS, D), PROMPT_BLOCKS * BLK, jnp.int32)
        end = jnp.int32(PROMPT_BLOCKS * BLK)
        for n in range(resp_ref.shape[0]):
            end = end + resp_ref[n]
            start = jnp.where(q_pos >= end, end, start)
        start = jnp.where(o < 2, 0, start)
        for b in range(BAND_BLOCKS):
            key_pos = lane + (band_start(o) + b) * BLK
            allowed = (key_pos >= start) & (key_pos <= q_pos)
            bias[o, :, pl.ds(b * BLK, BLK)] = jnp.where(allowed, 0.0, NEG)
        return c

    lax.fori_loop(0, NZ, masks, 0)

    landed(vstage, v_recv)
    for move in v_moves:
        send(*move)
    for move in q1_moves[2:]:
        remote(*move).start()
    forward(0)
    forward(1)

    primary = lax.rem(h, 2) == lax.rem(my_src, 2)
    which = lax.rem(h // 2 + my_src // 2, 2)

    def piece(w, s):
        return kv.at[w, pl.ds(NB * s, NB)]

    def x_move(s):
        src = piece(which, s)
        return (src, src, x_send.at[s], x_recv.at[s], z, x_peer)

    def c_move(w, s):
        src = piece(w, s)
        return (src, src, c_send.at[w, s], c_recv, z, c_peer)

    def source(t):
        return lax.rem(z + 4 + ((t + 1) // 2) * (1 - 2 * lax.rem(t, 2)), NZ)

    @pl.when(primary)
    def _():
        def own(t, c):
            s = source(NZ - 1 - t)
            landed(piece(which, s), z_recv.at[s])
            remote(*x_move(s)).start()
            remote(*c_move(which, s)).start()
            return c

        lax.fori_loop(0, NZ, own, 0)

    forward(2)
    forward(3)

    @pl.when(primary)
    def _():
        def other(t, c):
            s = source(NZ - 1 - t)
            landed(piece(1 - which, s), x_recv.at[s])
            remote(*c_move(1 - which, s)).start()
            return c

        lax.fori_loop(0, NZ, other, 0)

    @pl.when(jnp.logical_not(primary))
    def _():
        landed(kv, c_recv)

    def build(p, c):
        j = inv_ref[p]
        at = pl.ds(pl.multiple_of(p * BLK, BLK), BLK)
        kseq[:, at] = kv[0, j].T
        vseq[at, :] = kv[1, j]
        return c

    lax.fori_loop(0, NBLK, build, 0)

    out_col = my_k * WIDTH

    def o_move(c, o):
        first, last = CHUNKS[c]
        size = (last - first) * D
        cols = pl.ds(pl.multiple_of(out_col + first * D, D), size)
        src = obuf.at[o, :, :, pl.ds(first * D, size)]
        return (src, out_ref.at[:, :, cols], o_send.at[c, o], o_recv, o)

    def attend(t, o, spans):
        idx = [inv_ref[NB * o + b] for b in range(NB)]
        tile = jnp.zeros((ROWS, D), jnp.float32)
        for c, (begin, end) in enumerate(CHUNKS):
            n = end - begin
            q = jnp.concatenate(
                [qbuf[j, :, pl.ds(g * D, D)] for g in range(begin, end) for j in idx], axis=0
            )
            scores = []
            for at, use_bias in spans:
                s = jnp.dot(q, kseq[:, at], preferred_element_type=jnp.float32)
                if use_bias:
                    mask = bias[o, :, pl.ds(0, s.shape[1])]
                    s = (s.reshape(n, ROWS, -1) + mask[None]).reshape(s.shape)
                scores.append(s)
            top = functools.reduce(jnp.maximum, [jnp.max(s, axis=1, keepdims=True) for s in scores])
            total = jnp.zeros((n * ROWS, 1), jnp.float32)
            acc = jnp.zeros((n * ROWS, D), jnp.float32)
            for (at, _), s in zip(spans, scores):
                w = jnp.exp2((s - top) * (SCALE * LOG2E))
                total = total + jnp.sum(w, axis=1, keepdims=True)
                acc = acc + jnp.dot(
                    w.astype(jnp.bfloat16), vseq[at, :], preferred_element_type=jnp.float32
                )
            res = (acc / total).astype(jnp.bfloat16)
            lse = top * SCALE + jnp.log(total)
            for i in range(n):
                for b in range(NB):
                    first = i * ROWS + b * SUB
                    obuf[o, b, :, pl.ds((begin + i) * D, D)] = res[first : first + SUB]
                tile = jnp.where(lane == begin + i, lse[i * ROWS : (i + 1) * ROWS], tile)

            @pl.when(t < HELD)
            def _():
                send(*o_move(c, o))

        tile = jnp.concatenate([tile, jnp.zeros((D - ROWS, D), jnp.float32)], axis=0).T[:8]
        for b in range(NB):
            lse_seq[NB * o + b] = tile if b == 0 else pltpu.roll(tile, D - SUB * b, 1)

    landed(qbuf, q2_recv)

    def owner(t, carry):
        o = source(t)

        @pl.when(o < 2)
        def _():
            attend(t, o, [(pl.ds(0, PROMPT_BLOCKS * BLK), True)])

        @pl.when(o >= 2)
        def _():
            first = pl.multiple_of(band_start(o) * BLK, BLK)
            attend(t, o, [
                (pl.ds(0, PROMPT_BLOCKS * BLK), False),
                (pl.ds(first, BAND_BLOCKS * BLK), True),
            ])

        return carry

    lax.fori_loop(0, NZ, owner, 0)

    lane8 = lax.broadcasted_iota(jnp.int32, (8, D), 1)

    def l_move(s):
        return (lse_send.at[s], lse_recv.at[h, lax.rem(my_k, 2)], l_send.at[s], l_recv, s, my_src)

    for s in range(NZ):
        tile = lse_seq[order_ref[NB * s]]
        for b in range(1, NB):
            tile = jnp.where(
                lane8 >= SUB * b, pltpu.roll(lse_seq[order_ref[NB * s + b]], SUB * b, 1), tile
            )
        lse_send[s] = tile
        send(*l_move(s))

    def rest(t, carry):
        for c in range(len(CHUNKS)):
            send(*o_move(c, source(t)))
        return carry

    lax.fori_loop(HELD, NZ, rest, 0)
    landed(lse_recv, l_recv)
    for kk in range(2):
        for b in range(NB):
            tile = jnp.zeros((8, D), jnp.float32)
            for r in range(NH):
                shift = (SUB * (r - b)) % D
                part = lse_recv[r, kk]
                part = pltpu.roll(part, shift, 1) if shift else part
                tile = jnp.where(lane8 >= SUB * r, part, tile)
            lse_ref[pl.ds(kk * GROUP, GROUP), pl.ds(b * BLK, BLK)] = tile[:GROUP]

    remote(*v_move).wait_send()
    for move in k_moves + v_moves + q2_moves:
        sent(*move)
    for move in q1_moves:
        remote(*move).wait_send()

    @pl.when(primary)
    def _():
        def done(s, c):
            remote(*x_move(s)).wait_send()
            remote(*c_move(0, s)).wait_send()
            remote(*c_move(1, s)).wait_send()
            return c

        lax.fori_loop(0, NZ, done, 0)

    for s in range(NZ):
        sent(*l_move(jnp.int32(s)))
        for c in range(2):
            sent(*o_move(c, jnp.int32(s)))
    landed(out_ref, o_recv)


def solution(mesh):
    def step(q, k, v, order, resp):
        q = q.reshape(NB, BLK, q.shape[1])
        k = k.reshape(NB, BLK, k.shape[1])
        v = v.reshape(NB, BLK, v.shape[1])
        smem = pl.BlockSpec(memory_space=pltpu.SMEM)
        hbm = pl.BlockSpec(memory_space=pl.ANY)
        vmem = pl.BlockSpec(memory_space=pltpu.VMEM)
        dma = pltpu.SemaphoreType.DMA
        bf16 = lambda *shape: pltpu.VMEM(shape, jnp.bfloat16)
        f32 = lambda *shape: pltpu.VMEM(shape, jnp.float32)
        return pl.pallas_call(
            kernel,
            out_shape=(
                jax.ShapeDtypeStruct((NB, SUB, NZ * WIDTH), jnp.bfloat16),
                jax.ShapeDtypeStruct((2 * GROUP, NB * BLK), jnp.float32),
            ),
            in_specs=[smem, smem, hbm, hbm, hbm],
            out_specs=(hbm, vmem),
            scratch_shapes=[
                bf16(NB, BLK, 2 * D),
                bf16(NH, NB, SUB, 2 * WIDTH),
                bf16(2, NBLK, BLK, D),
                bf16(D, NBLK * BLK),
                bf16(NBLK * BLK, D),
                bf16(NBLK, SUB, WIDTH),
                bf16(NZ, NB, SUB, WIDTH),
                f32(NZ, ROWS, BAND_BLOCKS * BLK),
                f32(NBLK, 8, D),
                f32(NZ, 8, D),
                f32(NH, 2, 8, D),
                pltpu.SMEM((NBLK,), jnp.int32),
                dma((4,)), dma, dma((2, NH - 1)), dma((NH, 2)), dma((NZ,)), dma((2, NZ)),
                dma((2, NZ)), dma((NZ,)),
                dma, dma((2, NH)), dma, dma((NZ,)), dma((NZ,)), dma, dma, dma,
            ],
            compiler_params=pltpu.CompilerParams(
                collective_id=0, has_side_effects=True, vmem_limit_bytes=60 << 20
            ),
        )(order, resp, q, k, v)

    rows = P(("dp", "ctx"), "head")
    return jax.shard_map(
        step,
        mesh=mesh,
        in_specs=(rows, rows, rows, P("dp"), P("dp")),
        out_specs=(P(("dp", "ctx"), "head", None), P("head", ("dp", "ctx"))),
        check_vma=False,
    )
```

time: 85.6 us -> 75.9 us (0.89)
  Pallas kernels: 82.1 us -> 72.3 us
    pallas_call x1, Pallas kernels: 82.1 us -> 72.3 us  [step(): pl.pallas_call(kernel, out_shape=(jax.ShapeDtypeStruct((NB, SUB, NZ * WID...]
where the time goes in v3:
time: 75.9 us; the launch traced here: 75.7 us
  Pallas kernels  72.3 us (95%)
  local copies, waits for them, and re-layouts  2.83 us (4%)
    pallas_call x1, Pallas kernels, step(): pl.pallas_call(kernel, out_shape=(jax.ShapeDtypeStruct((NB, SUB, NZ * WID...  72.3 us
    unnamed x4, local copies, waits for them, and re-layouts  2.83 us

profile of v3, /device:TPU:1, one launch (start us, length us, event | category | flops | bytes accessed | tf_op | source)
XLA Modules:
  0.0 75.7 jit_solution(13688330343462254799)
XLA Ops:
  0.6 72.3 %shard_map.68 = (bf16[3,32,5120]{2,1,0:T(8,128)(2,1)}, f32[10,384]{1,0:T(8,128)}) custom-call(s32[24]{0:T(128)} %order_ref.1, s32[16]{0:T(128)} %resp_ref.1, bf16[3,128,1280]{2,1,0:T(8,128)(2,1)} %bitcast.3, bf16[3,128,256]{2,1,0:T(8,128)(2,1)} %bitcast.4, bf16[3,128,256]{2,1,0:T(8,128)(2,1)} %bitcast.5), custom_call_target="tpu_custom_call" | custom-call | tf_op jit(solution)/shard_map/pallas_call | solution.py:372
  72.9 0.0 copy-start
  72.9 2.2 %copy.9 = bf16[3,32,5120]{2,1,0:T(8,128)(2,1)} copy(bf16[3,32,5120]{2,1,0:T(8,128)(2,1)} %get-tuple-element.4) | data formatting | bytes 1966080
  75.1 0.0 copy-done
  75.1 0.6 copy.10
Async XLA Ops:
  72.9 2.2 %copy-start = (f32[10,384]{1,0:T(8,128)S(1)}, f32[10,384]{1,0:T(8,128)}, u32[]{:S(2)}) copy-start(f32[10,384]{1,0:T(8,128)} %get-tuple-element.5) | copy-start | bytes 46084

commit v4 on v3

--- a/solution.py
+++ b/solution.py
@@ -25,12 +25,11 @@
 SCALE = 1.0 / math.sqrt(D)
 LOG2E = 1.4426950408889634
 NEG = -1e30
-HELD = 5
 
 
 def kernel(
     order_ref, resp_ref, q_ref, k_ref, v_ref, out_ref, lse_ref,
-    vstage, qstage, kv, kseq, vseq, qbuf, obuf, bias,
+    vstage, qstage, kv, kseq, vseq, qbuf_a, qbuf_b, obuf, bias,
     lse_seq, lse_send, lse_recv, inv_ref,
     kv_send, v_send, q1_send, q2_send, x_send, c_send, o_send, l_send,
     v_recv, q1_recv, q2_recv, z_recv, x_recv, c_recv, o_recv, l_recv,
@@ -41,6 +40,7 @@
     c_peer = h + 1 - 2 * lax.rem(h, 2)
     d_peer = lax.rem(c_peer + 2, NH)
     peers = (c_peer, x_peer, d_peer)
+    qbuf = (qbuf_a, qbuf_b)
 
     def plane(k):
         return lax.rem(2 * k, NZ) + k // 4
@@ -103,42 +103,56 @@
          plane(2 * x_peer + kk))
         for kk in range(2)
     ]
-    v_move = (v_ref, vstage, v_send, v_recv, z, x_peer)
-    remote(*v_move).start()
+    v1_moves = [
+        (v_ref.at[:, :, pl.ds(D * kk, D)], vstage.at[:, :, pl.ds(D * kk, D)],
+         v_send.at[kk], v_recv.at[kk], z, x_peer)
+        for kk in range(2)
+    ]
+    for move in v1_moves:
+        remote(*move).start()
     for move in k_moves:
         send(*move)
 
-    def q_cols(kk):
-        return pl.ds(WIDTH * kk, WIDTH)
-
-    def q1_move(e, kk):
+    def q_cols(c, kk):
+        first, last = CHUNKS[c]
+        return pl.ds(WIDTH * kk + D * first, D * (last - first))
+
+    def q1_move(c, kk, e):
         rows = pl.ds(pl.multiple_of(SUB * peers[e], SUB), SUB)
+        n = 2 * c + kk
         return (
-            q_ref.at[:, rows, q_cols(kk)], qstage.at[h, :, :, q_cols(kk)],
-            q1_send.at[kk, e], q1_recv.at[kk, h], z, peers[e],
+            q_ref.at[:, rows, q_cols(c, kk)], qstage.at[h, :, :, q_cols(c, kk)],
+            q1_send.at[n, e], q1_recv.at[n, h], z, peers[e],
         )
 
-    q1_moves = [q1_move(e, kk) for e in range(NH - 1) for kk in range(2)]
-    for move in q1_moves[:2]:
-        remote(*move).start()
-
-    def q2_move(e, hd, kk):
+    q1_moves = [q1_move(c, kk, e) for c in range(2) for kk in range(2) for e in range(NH - 1)]
+
+    def share_queries(c, *where):
+        for e in where:
+            for kk in range(2):
+                remote(*q1_move(c, kk, e)).start()
+
+    def q2_move(c, e, kk):
+        hd = (h, *peers)[e]
         if e == 0:
-            src = q_ref.at[:, pl.ds(pl.multiple_of(SUB * h, SUB), SUB), q_cols(kk)]
+            src = q_ref.at[:, pl.ds(pl.multiple_of(SUB * h, SUB), SUB), q_cols(c, kk)]
         else:
-            src = qstage.at[hd, :, :, q_cols(kk)]
-        return (src, qbuf.at[here], q2_send.at[e, kk], q2_recv, plane(2 * hd + kk))
-
-    q2_moves = []
-
-    def forward(e):
-        hd = (h, *peers)[e]
+            src = qstage.at[hd, :, :, q_cols(c, kk)]
+        return (
+            src, qbuf[c].at[here], q2_send.at[c, 2 * e + kk], q2_recv.at[c], plane(2 * hd + kk),
+        )
+
+    q2_moves = [q2_move(c, e, kk) for c in range(2) for e in range(NH) for kk in range(2)]
+
+    def forward(c, e):
         for kk in range(2):
-            move = q2_move(e, hd, kk)
+            move = q2_move(c, e, kk)
             if e:
-                landed(move[0], q1_recv.at[kk, hd])
+                landed(move[0], q1_recv.at[2 * c + kk, (h, *peers)[e]])
             send(*move)
-            q2_moves.append(move)
+
+    share_queries(0, 0)
+    share_queries(1, 0)
 
     def find(p, c):
         found = jnp.int32(0)
@@ -172,13 +186,12 @@
 
     lax.fori_loop(0, NZ, masks, 0)
 
-    landed(vstage, v_recv)
-    for move in v_moves:
-        send(*move)
-    for move in q1_moves[2:]:
-        remote(*move).start()
-    forward(0)
-    forward(1)
+    for kk in range(2):
+        landed(v_moves[kk][0], v_recv.at[kk])
+        send(*v_moves[kk])
+    share_queries(0, 1, 2)
+    forward(0, 0)
+    forward(0, 1)
 
     primary = lax.rem(h, 2) == lax.rem(my_src, 2)
     which = lax.rem(h // 2 + my_src // 2, 2)
@@ -208,8 +221,11 @@
 
         lax.fori_loop(0, NZ, own, 0)
 
-    forward(2)
-    forward(3)
+    forward(0, 2)
+    forward(0, 3)
+    share_queries(1, 1, 2)
+    forward(1, 0)
+    forward(1, 1)
 
     @pl.when(primary)
     def _():
@@ -221,6 +237,9 @@
 
         lax.fori_loop(0, NZ, other, 0)
 
+    forward(1, 2)
+    forward(1, 3)
+
     @pl.when(jnp.logical_not(primary))
     def _():
         landed(kv, c_recv)
@@ -243,66 +262,64 @@
         src = obuf.at[o, :, :, pl.ds(first * D, size)]
         return (src, out_ref.at[:, :, cols], o_send.at[c, o], o_recv, o)
 
-    def attend(t, o, spans):
+    def attend(c, o, spans):
         idx = [inv_ref[NB * o + b] for b in range(NB)]
+        begin, end = CHUNKS[c]
+        n = end - begin
+        q = jnp.concatenate(
+            [qbuf[c][j, :, pl.ds(g * D, D)] for g in range(n) for j in idx], axis=0
+        )
+        scores = []
+        for at, use_bias in spans:
+            s = jnp.dot(q, kseq[:, at], preferred_element_type=jnp.float32)
+            if use_bias:
+                mask = bias[o, :, pl.ds(0, s.shape[1])]
+                s = (s.reshape(n, ROWS, -1) + mask[None]).reshape(s.shape)
+            scores.append(s)
+        top = functools.reduce(jnp.maximum, [jnp.max(s, axis=1, keepdims=True) for s in scores])
+        total = jnp.zeros((n * ROWS, 1), jnp.float32)
+        acc = jnp.zeros((n * ROWS, D), jnp.float32)
+        for (at, _), s in zip(spans, scores):
+            w = jnp.exp2((s - top) * (SCALE * LOG2E))
+            total = total + jnp.sum(w, axis=1, keepdims=True)
+            acc = acc + jnp.dot(
+                w.astype(jnp.bfloat16), vseq[at, :], preferred_element_type=jnp.float32
+            )
+        res = (acc / total).astype(jnp.bfloat16)
+        lse = top * SCALE + jnp.log(total)
         tile = jnp.zeros((ROWS, D), jnp.float32)
-        for c, (begin, end) in enumerate(CHUNKS):
-            n = end - begin
-            q = jnp.concatenate(
-                [qbuf[j, :, pl.ds(g * D, D)] for g in range(begin, end) for j in idx], axis=0
-            )
-            scores = []
-            for at, use_bias in spans:
-                s = jnp.dot(q, kseq[:, at], preferred_element_type=jnp.float32)
-                if use_bias:
-                    mask = bias[o, :, pl.ds(0, s.shape[1])]
-                    s = (s.reshape(n, ROWS, -1) + mask[None]).reshape(s.shape)
-                scores.append(s)
-            top = functools.reduce(jnp.maximum, [jnp.max(s, axis=1, keepdims=True) for s in scores])
-            total = jnp.zeros((n * ROWS, 1), jnp.float32)
-            acc = jnp.zeros((n * ROWS, D), jnp.float32)
-            for (at, _), s in zip(spans, scores):
-                w = jnp.exp2((s - top) * (SCALE * LOG2E))
-                total = total + jnp.sum(w, axis=1, keepdims=True)
-                acc = acc + jnp.dot(
-                    w.astype(jnp.bfloat16), vseq[at, :], preferred_element_type=jnp.float32
-                )
-            res = (acc / total).astype(jnp.bfloat16)
-            lse = top * SCALE + jnp.log(total)
-            for i in range(n):
-                for b in range(NB):
-                    first = i * ROWS + b * SUB
-                    obuf[o, b, :, pl.ds((begin + i) * D, D)] = res[first : first + SUB]
-                tile = jnp.where(lane == begin + i, lse[i * ROWS : (i + 1) * ROWS], tile)
-
-            @pl.when(t < HELD)
-            def _():
-                send(*o_move(c, o))
-
+        for i in range(n):
+            for b in range(NB):
+                first = i * ROWS + b * SUB
+                obuf[o, b, :, pl.ds((begin + i) * D, D)] = res[first : first + SUB]
+            tile = jnp.where(lane == begin + i, lse[i * ROWS : (i + 1) * ROWS], tile)
         tile = jnp.concatenate([tile, jnp.zeros((D - ROWS, D), jnp.float32)], axis=0).T[:8]
         for b in range(NB):
-            lse_seq[NB * o + b] = tile if b == 0 else pltpu.roll(tile, D - SUB * b, 1)
-
-    landed(qbuf, q2_recv)
-
-    def owner(t, carry):
-        o = source(t)
-
-        @pl.when(o < 2)
-        def _():
-            attend(t, o, [(pl.ds(0, PROMPT_BLOCKS * BLK), True)])
-
-        @pl.when(o >= 2)
-        def _():
-            first = pl.multiple_of(band_start(o) * BLK, BLK)
-            attend(t, o, [
-                (pl.ds(0, PROMPT_BLOCKS * BLK), False),
-                (pl.ds(first, BAND_BLOCKS * BLK), True),
-            ])
-
-        return carry
-
-    lax.fori_loop(0, NZ, owner, 0)
+            part = tile if b == 0 else pltpu.roll(tile, D - SUB * b, 1)
+            lse_seq[NB * o + b] = part if c == 0 else part + lse_seq[NB * o + b]
+
+    for c in range(2):
+        landed(qbuf[c], q2_recv.at[c])
+
+        def owner(t, carry, c=c):
+            o = source(t)
+
+            @pl.when(o < 2)
+            def _():
+                attend(c, o, [(pl.ds(0, PROMPT_BLOCKS * BLK), True)])
+
+            @pl.when(o >= 2)
+            def _():
+                first = pl.multiple_of(band_start(o) * BLK, BLK)
+                attend(c, o, [
+                    (pl.ds(0, PROMPT_BLOCKS * BLK), False),
+                    (pl.ds(first, BAND_BLOCKS * BLK), True),
+                ])
+
+            send(*o_move(c, o))
+            return carry
+
+        lax.fori_loop(0, NZ, owner, 0)
 
     lane8 = lax.broadcasted_iota(jnp.int32, (8, D), 1)
 
@@ -318,12 +335,6 @@
         lse_send[s] = tile
         send(*l_move(s))
 
-    def rest(t, carry):
-        for c in range(len(CHUNKS)):
-            send(*o_move(c, source(t)))
-        return carry
-
-    lax.fori_loop(HELD, NZ, rest, 0)
     landed(lse_recv, l_recv)
     for kk in range(2):
         for b in range(NB):
@@ -335,7 +346,8 @@
                 tile = jnp.where(lane8 >= SUB * r, part, tile)
             lse_ref[pl.ds(kk * GROUP, GROUP), pl.ds(b * BLK, BLK)] = tile[:GROUP]
 
-    remote(*v_move).wait_send()
+    for move in v1_moves:
+        remote(*move).wait_send()
     for move in k_moves + v_moves + q2_moves:
         sent(*move)
     for move in q1_moves:
@@ -383,16 +395,16 @@
                 bf16(2, NBLK, BLK, D),
                 bf16(D, NBLK * BLK),
                 bf16(NBLK * BLK, D),
-                bf16(NBLK, SUB, WIDTH),
+                *[bf16(NBLK, SUB, D * (last - first)) for first, last in CHUNKS],
                 bf16(NZ, NB, SUB, WIDTH),
                 f32(NZ, ROWS, BAND_BLOCKS * BLK),
                 f32(NBLK, 8, D),
                 f32(NZ, 8, D),
                 f32(NH, 2, 8, D),
                 pltpu.SMEM((NBLK,), jnp.int32),
-                dma((4,)), dma, dma((2, NH - 1)), dma((NH, 2)), dma((NZ,)), dma((2, NZ)),
+                dma((4,)), dma((2,)), dma((4, NH - 1)), dma((2, NZ)), dma((NZ,)), dma((2, NZ)),
                 dma((2, NZ)), dma((NZ,)),
-                dma, dma((2, NH)), dma, dma((NZ,)), dma((NZ,)), dma, dma, dma,
+                dma((2,)), dma((4, NH)), dma((2,)), dma((NZ,)), dma((NZ,)), dma, dma, dma,
             ],
             compiler_params=pltpu.CompilerParams(
                 collective_id=0, has_side_effects=True, vmem_limit_bytes=60 << 20

time: 75.9 us -> 72.8 us (0.959); the launches traced: 75.7 us -> 71.6 us
  Pallas kernels: 72.3 us -> 68.1 us
    pallas_call x1, Pallas kernels: 72.3 us -> 68.1 us  [step(): pl.pallas_call(kernel, out_shape=(jax.ShapeDtypeStruct((NB, SUB, NZ * WID...]
where the time goes in v4:
time: 72.8 us; the launch traced here: 71.6 us
  Pallas kernels  68.1 us (94%)
  local copies, waits for them, and re-layouts  2.83 us (4%)
    pallas_call x1, Pallas kernels, step(): pl.pallas_call(kernel, out_shape=(jax.ShapeDtypeStruct((NB, SUB, NZ * WID...  68.1 us
    unnamed x4, local copies, waits for them, and re-layouts  2.83 us

profile of v4, /device:TPU:1, one launch (start us, length us, event | category | flops | bytes accessed | tf_op | source)
XLA Modules:
  0.0 71.6 jit_solution(2124044181214761004)
XLA Ops:
  0.6 68.1 %shard_map.68 = (bf16[3,32,5120]{2,1,0:T(8,128)(2,1)}, f32[10,384]{1,0:T(8,128)}) custom-call(s32[24]{0:T(128)} %order_ref.1, s32[16]{0:T(128)} %resp_ref.1, bf16[3,128,1280]{2,1,0:T(8,128)(2,1)} %bitcast.3, bf16[3,128,256]{2,1,0:T(8,128)(2,1)} %bitcast.4, bf16[3,128,256]{2,1,0:T(8,128)(2,1)} %bitcast.5), custom_call_target="tpu_custom_call" | custom-call | tf_op jit(solution)/shard_map/pallas_call | solution.py:384
  68.8 0.0 copy-start
  68.8 2.2 %copy.9 = bf16[3,32,5120]{2,1,0:T(8,128)(2,1)} copy(bf16[3,32,5120]{2,1,0:T(8,128)(2,1)} %get-tuple-element.4) | data formatting | bytes 1966080
  71.0 0.0 copy-done
  71.0 0.6 copy.10
Async XLA Ops:
  68.8 2.2 %copy-start = (f32[10,384]{1,0:T(8,128)S(1)}, f32[10,384]{1,0:T(8,128)}, u32[]{:S(2)}) copy-start(f32[10,384]{1,0:T(8,128)} %get-tuple-element.5) | copy-start | bytes 46084

commit v5 on v4

--- a/solution.py
+++ b/solution.py
@@ -370,6 +370,19 @@
     landed(out_ref, o_recv)
 
 
+def finish(out_ref, lse_ref, out, lse, out_v, lse_v, sem, sem2):
+    pairs = [(out_ref.at[b], out_v.at[b], out.at[b]) for b in range(NB)] + [(lse_ref, lse_v, lse)]
+    ins = [pltpu.make_async_copy(p[0], p[1], sem.at[i]) for i, p in enumerate(pairs)]
+    outs = [pltpu.make_async_copy(p[1], p[2], sem2.at[i]) for i, p in enumerate(pairs)]
+    for copy in ins:
+        copy.start()
+    for i, o in zip(ins, outs):
+        i.wait()
+        o.start()
+    for o in outs:
+        o.wait()
+
+
 def solution(mesh):
     def step(q, k, v, order, resp):
         q = q.reshape(NB, BLK, q.shape[1])
@@ -381,7 +394,7 @@
         dma = pltpu.SemaphoreType.DMA
         bf16 = lambda *shape: pltpu.VMEM(shape, jnp.bfloat16)
         f32 = lambda *shape: pltpu.VMEM(shape, jnp.float32)
-        return pl.pallas_call(
+        out, lse = pl.pallas_call(
             kernel,
             out_shape=(
                 jax.ShapeDtypeStruct((NB, SUB, NZ * WIDTH), jnp.bfloat16),
@@ -410,6 +423,22 @@
                 collective_id=0, has_side_effects=True, vmem_limit_bytes=60 << 20
             ),
         )(order, resp, q, k, v)
+        return pl.pallas_call(
+            finish,
+            out_shape=(
+                jax.ShapeDtypeStruct(out.shape, out.dtype),
+                jax.ShapeDtypeStruct(lse.shape, lse.dtype),
+            ),
+            in_specs=[hbm, hbm],
+            out_specs=(hbm, hbm),
+            scratch_shapes=[
+                pltpu.VMEM(out.shape, out.dtype),
+                pltpu.VMEM(lse.shape, lse.dtype),
+                dma((NB + 1,)),
+                dma((NB + 1,)),
+            ],
+            compiler_params=pltpu.CompilerParams(vmem_limit_bytes=60 << 20),
+        )(out, lse)
 
     rows = P(("dp", "ctx"), "head")
     return jax.shard_map(

time: 72.8 us -> 71.9 us (0.988)
  local copies, waits for them, and re-layouts: 2.83 us -> 0 us
  Pallas kernels: 68.1 us -> 70.1 us
    unnamed x4 -> x0, local copies, waits for them, and re-layouts: 2.83 us -> none
    pallas_call x0 -> x1, Pallas kernels: none -> 1.98 us  [step(): pl.pallas_call(finish, out_shape=(jax.ShapeDtypeStruct(out.shape, out.dty...]
where the time goes in v5:
time: 71.9 us; the launch traced here: 70.8 us
  Pallas kernels  70.1 us (97%)
    pallas_call x1, Pallas kernels, step(): pl.pallas_call(kernel, out_shape=(jax.ShapeDtypeStruct((NB, SUB, NZ * WID...  68.1 us
    pallas_call x1, Pallas kernels, step(): pl.pallas_call(finish, out_shape=(jax.ShapeDtypeStruct(out.shape, out.dty...  1.98 us

profile of v5, /device:TPU:1, one launch (start us, length us, event | category | flops | bytes accessed | tf_op | source)
XLA Modules:
  0.0 70.8 jit_solution(7813125545322672341)
XLA Ops:
  0.6 68.1 %shard_map.68 = (bf16[3,32,5120]{2,1,0:T(8,128)(2,1)}, f32[10,384]{1,0:T(8,128)}) custom-call(s32[24]{0:T(128)} %order_ref.1, s32[16]{0:T(128)} %resp_ref.1, bf16[3,128,1280]{2,1,0:T(8,128)(2,1)} %bitcast.3, bf16[3,128,256]{2,1,0:T(8,128)(2,1)} %bitcast.4, bf16[3,128,256]{2,1,0:T(8,128)(2,1)} %bitcast.5), custom_call_target="tpu_custom_call" | custom-call | tf_op jit(solution)/shard_map/pallas_call | solution.py:397
  68.8 2.0 %shard_map.69 = (bf16[3,32,5120]{2,1,0:T(8,128)(2,1)}, f32[10,384]{1,0:T(8,128)}) custom-call(bf16[3,32,5120]{2,1,0:T(8,128)(2,1)} %get-tuple-element.4.out_ref, f32[10,384]{1,0:T(8,128)} %get-tuple-element.5.lse_ref), custom_call_target="tpu_custom_call" | custom-call | tf_op jit(solution)/shard_map/pallas_call | solution.py:426

commit v6 on v5

--- a/solution.py
+++ b/solution.py
@@ -49,7 +49,7 @@
     my_src = my_k // 2
 
     barrier = pltpu.get_barrier_semaphore()
-    for dz in range(1, NZ):
+    for dz in (4, 3, 5, 2, 6, 1, 7):
         pl.semaphore_signal(
             barrier, inc=1, device_id={"ctx": lax.rem(z + dz, NZ)}, device_id_type=MESH
         )
@@ -154,6 +154,13 @@
     share_queries(0, 0)
     share_queries(1, 0)
 
+    for kk in range(2):
+        landed(v_moves[kk][0], v_recv.at[kk])
+        send(*v_moves[kk])
+    share_queries(0, 1, 2)
+    forward(0, 0)
+    forward(0, 1)
+
     def find(p, c):
         found = jnp.int32(0)
         for j in range(NBLK):
@@ -186,13 +193,6 @@
 
     lax.fori_loop(0, NZ, masks, 0)
 
-    for kk in range(2):
-        landed(v_moves[kk][0], v_recv.at[kk])
-        send(*v_moves[kk])
-    share_queries(0, 1, 2)
-    forward(0, 0)
-    forward(0, 1)
-
     primary = lax.rem(h, 2) == lax.rem(my_src, 2)
     which = lax.rem(h // 2 + my_src // 2, 2)
 
@@ -216,7 +216,6 @@
             s = source(NZ - 1 - t)
             landed(piece(which, s), z_recv.at[s])
             remote(*x_move(s)).start()
-            remote(*c_move(which, s)).start()
             return c
 
         lax.fori_loop(0, NZ, own, 0)
@@ -232,6 +231,7 @@
         def other(t, c):
             s = source(NZ - 1 - t)
             landed(piece(1 - which, s), x_recv.at[s])
+            remote(*c_move(which, s)).start()
             remote(*c_move(1 - which, s)).start()
             return c
 

time: 71.9 us -> 71.9 us (level)
  no operation moved by 1% of the time
where the time goes in v6:
time: 71.9 us; the launch traced here: 70.8 us
  Pallas kernels  70.1 us (97%)
    pallas_call x1, Pallas kernels, step(): pl.pallas_call(kernel, out_shape=(jax.ShapeDtypeStruct((NB, SUB, NZ * WID...  68.2 us
    pallas_call x1, Pallas kernels, step(): pl.pallas_call(finish, out_shape=(jax.ShapeDtypeStruct(out.shape, out.dty...  1.98 us

profile of v6, /device:TPU:1, one launch (start us, length us, event | category | flops | bytes accessed | tf_op | source)
XLA Modules:
  0.0 70.8 jit_solution(11801800327139533127)
XLA Ops:
  0.6 68.2 %shard_map.68 = (bf16[3,32,5120]{2,1,0:T(8,128)(2,1)}, f32[10,384]{1,0:T(8,128)}) custom-call(s32[24]{0:T(128)} %order_ref.1, s32[16]{0:T(128)} %resp_ref.1, bf16[3,128,1280]{2,1,0:T(8,128)(2,1)} %bitcast.3, bf16[3,128,256]{2,1,0:T(8,128)(2,1)} %bitcast.4, bf16[3,128,256]{2,1,0:T(8,128)(2,1)} %bitcast.5), custom_call_target="tpu_custom_call" | custom-call | tf_op jit(solution)/shard_map/pallas_call | solution.py:397
  68.8 2.0 %shard_map.69 = (bf16[3,32,5120]{2,1,0:T(8,128)(2,1)}, f32[10,384]{1,0:T(8,128)}) custom-call(bf16[3,32,5120]{2,1,0:T(8,128)(2,1)} %get-tuple-element.4.out_ref, f32[10,384]{1,0:T(8,128)} %get-tuple-element.5.lse_ref), custom_call_target="tpu_custom_call" | custom-call | tf_op jit(solution)/shard_map/pallas_call | solution.py:426
